TPU v7x, 512 devices: a whole 4x4x16 slice. The times are simulated.
512 devices in a mesh: dp: 16 (over y, x_hi, core), slab: 32 (over z, x_lo).
Axes of the slice: x: 4 (x_hi: 2, x_lo: 2; x = x_hi * 2 + x_lo), y: 4, z: 16, core: 2. Of those that a mesh axis runs over, the one named last changes fastest.
Arguments:
- features: bfloat16 [16, 64, 256, 8, 256], P('dp', None, 'slab'), may hold values from -6 to 6
- target: bfloat16 [16, 256, 8, 256], P('dp', 'slab'), may hold values from -6 to 6
- out_weight: float32 [64], replicated, may hold values from -1.5 to 1.5
- rotation: int32 [16], P('dp'), may hold values from 0 to 3
- blocks: int32 [8, 2], replicated, may hold values from 0 to 3, as said below
- wedge: int32 [256, 256], replicated, may hold values 0 or 1
Outputs:
- vol_grad: float32 [16, 256, 8, 256], P('dp', 'slab')
- w_grad: float32 [64], replicated
Inputs may be any that keep to these rules, and one draw needn't show every extreme that they name: `blocks`: the 8 rows are distinct pairs of block indices of the frequency plane, each from 0 to 3.
All inputs are finite; a program needn't handle non-finite values.
Results may differ from a plain program's by a relative error of at most 0.0003.
Values sent between devices are 32-bit elements; how exact they have to be, the bound alone decides.
No kernel may reach another device: no remote copies, remote signals or barrier semaphores. Data moves between devices by JAX's collectives and lax.ppermute only.
A program may use at most 64 MiB of HBM per device.

v0:
```python
import math

import jax
import jax.numpy as jnp
from jax import lax
from jax.sharding import PartitionSpec as P

BLK = 64


def product(form, left, right):
    return jnp.einsum(form, left, right, precision=lax.Precision.HIGHEST)


def wedge_weights(blocks, wedge, length):
    per_side = length // BLK
    labels = jnp.arange(per_side, dtype=jnp.int32)
    match = (blocks[:, 0][:, None, None] == labels[None, :, None]) & (
        blocks[:, 1][:, None, None] == labels[None, None, :]
    )
    listed = jnp.any(match, axis=0)
    spread = jnp.repeat(jnp.repeat(listed, BLK, axis=0), BLK, axis=1)
    return jnp.where(spread, wedge, 0).astype(jnp.float32)


def phase_tables(turns, length):
    positions = jnp.arange(length, dtype=jnp.int32)
    flip_depth = turns >= 2
    flip_width = (turns == 1) | (turns == 2)
    depth_index = jnp.where(
        flip_depth[:, None], length - 1 - positions[None, :], positions[None, :]
    )
    width_index = jnp.where(
        flip_width[:, None], length - 1 - positions[None, :], positions[None, :]
    )
    depth_phase = positions[None, :, None] * depth_index[:, None, :] % length
    width_phase = width_index[:, :, None] * positions[None, None, :] % length
    depth_angle = depth_phase.astype(jnp.float32) * (2.0 * math.pi / length)
    width_angle = width_phase.astype(jnp.float32) * (2.0 * math.pi / length)
    return (jnp.cos(depth_angle), jnp.sin(depth_angle), jnp.cos(width_angle), jnp.sin(width_angle))


def on_device(features, target, out_weight, rotation, blocks, wedge):
    length = features.shape[-1]
    plane_count = features.shape[3]
    slab_count = lax.axis_size("slab")
    columns = length // slab_count
    col_start = lax.axis_index("slab") * columns
    features_wide = features.astype(jnp.float32)
    volume = product("c,sczyx->szyx", out_weight, features_wide)
    difference = volume - target.astype(jnp.float32)
    depth_cos, depth_sin, width_cos, width_sin = phase_tables(rotation, length)
    line_real = product("szyb,sbp->szyp", difference, width_cos)
    line_imag = -product("szyb,sbp->szyp", difference, width_sin)
    line_real, line_imag = (
        lax.all_to_all(line_real, "slab", split_axis=3, concat_axis=1, tiled=True),
        lax.all_to_all(line_imag, "slab", split_axis=3, concat_axis=1, tiled=True),
    )
    spec_real = (
        product("spa,sayq->spyq", depth_cos, line_real)
        + product("spa,sayq->spyq", depth_sin, line_imag)
    ) / length
    spec_imag = (
        product("spa,sayq->spyq", depth_cos, line_imag)
        - product("spa,sayq->spyq", depth_sin, line_real)
    ) / length
    mask = wedge_weights(blocks, wedge, length)
    odd_turn = rotation % 2 == 1
    mask_turned = jnp.where(odd_turn[:, None, None], mask.T[None], mask[None])
    mask_columns = lax.dynamic_slice_in_dim(mask_turned, col_start, columns, 2)
    grad_real = 2.0 * mask_columns[:, :, None, :] * spec_real
    grad_imag = 2.0 * mask_columns[:, :, None, :] * spec_imag
    back_real = product("spa,spyq->sayq", depth_cos, grad_real) - product(
        "spa,spyq->sayq", depth_sin, grad_imag
    )
    back_imag = product("spa,spyq->sayq", depth_cos, grad_imag) + product(
        "spa,spyq->sayq", depth_sin, grad_real
    )
    back_real, back_imag = (
        lax.all_to_all(back_real, "slab", split_axis=1, concat_axis=3, tiled=True),
        lax.all_to_all(back_imag, "slab", split_axis=1, concat_axis=3, tiled=True),
    )
    vol_grad = (
        product("sayp,sbp->sayb", back_real, width_cos)
        - product("sayp,sbp->sayb", back_imag, width_sin)
    ) / length
    voxel_count = lax.axis_size("dp") * features.shape[0] * length * plane_count * length
    local_sum = product("sczyx,szyx->c", features_wide, vol_grad) / voxel_count
    w_grad = lax.psum(local_sum, ("dp", "slab"))
    return (vol_grad, w_grad)


def solution(mesh):
    in_specs = (
        P("dp", None, "slab", None, None),
        P("dp", "slab", None, None),
        P(),
        P("dp"),
        P(),
        P(),
    )
    out_specs = (P("dp", "slab", None, None), P())
    return jax.shard_map(
        on_device, mesh=mesh, in_specs=in_specs, out_specs=out_specs, check_vma=False
    )
```

profile of v0, /device:TPU:1, one launch (start us, length us, event | category | flops | bytes accessed | tf_op | source)
XLA Modules:
  0.0 234.3 jit_solution(6017797362863965767)
XLA Ops:
  2.2 2.5 %fusion.2 = f32[1,8,8,256]{3,0,2,1:T(1,128)S(1)} fusion(bf16[64,8,8,256]{3,2,1,0:T(8,128)(2,1)S(1)} %bitcast.144, f32[64]{0:T(128)} %param.8), kind=kOutput, calls=%fused_computation.2 | convolution fusion | flops 12582912 | bytes 2162944 | tf_op jit(solution)/shard_map/c,sczyx->szyx/dot_general | solution.py:12
  7.6 17.1 %all-to-all-start = ((f32[32,1,512]{2,1,0:T(1,128)}), f32[32,1,512]{2,1,0:T(1,128)S(1)}, u32[]{:S(2)}, u32[]{:S(2)}) async-start(f32[32,1,512]{2,1,0:T(1,128)} %reshape.620), calls=%async_computation | async-start | bytes 131072 | tf_op jit(solution)/shard_map/all_to_all | solution.py:56
  24.7 2.7 %fusion.4 = f32[1,8,8,256]{3,2,1,0:T(8,128)} fusion(s32[256]{0:T(256)S(1)} %iota_select_fusion, f32[1,8,8,256]{3,0,2,1:T(1,128)S(1)} %fusion.2, bf16[1,8,8,256]{3,2,1,0:T(8,128)(2,1)} %param.7), kind=kOutput, calls=%fused_computation.12 | convolution fusion | flops 51298304 | bytes 164864 | tf_op jit(solution)/shard_map/szyb,sbp->szyp/dot_general | solution.py:12
  29.8 7.5 %all-to-all-done = f32[32,1,512]{2,1,0:T(1,128)S(1)} async-done(((f32[32,1,512]{2,1,0:T(1,128)}), f32[32,1,512]{2,1,0:T(1,128)S(1)}, u32[]{:S(2)}, u32[]{:S(2)}) %all-to-all-start) | async-done | bytes 65568 | tf_op jit(solution)/shard_map/all_to_all | solution.py:56
  37.3 5.3 %all-to-all-start.1 = ((f32[32,1,512]{2,1,0:T(1,128)}), f32[32,1,512]{2,1,0:T(1,128)S(1)}, u32[]{:S(2)}, u32[]{:S(2)}) async-start(f32[32,1,512]{2,1,0:T(1,128)} %reshape.622), calls=%async_computation.1 | async-start | bytes 131072 | tf_op jit(solution)/shard_map/all_to_all | solution.py:57
  45.3 1.7 copy.71
  47.0 2.1 copy.44
  49.7 5.2 %all-to-all-done.1 = f32[32,1,512]{2,1,0:T(1,128)S(1)} async-done(((f32[32,1,512]{2,1,0:T(1,128)}), f32[32,1,512]{2,1,0:T(1,128)S(1)}, u32[]{:S(2)}, u32[]{:S(2)}) %all-to-all-start.1) | async-done | bytes 65568 | tf_op jit(solution)/shard_map/all_to_all | solution.py:57
  56.3 1.7 copy.72
  58.0 2.1 copy.47
  64.7 1.4 convolution_bitcast_fusion.2
  66.1 13.9 %fusion.7 = f32[256,64]{0,1:T(8,128)S(1)} fusion(f32[256,8,8]{0,2,1:T(8,128)S(1)} %convolution_bitcast_fusion.6, f32[256,64]{0,1:T(8,128)S(1)} %reshape.597, s32[256]{0:T(256)S(1)} %iota_select_fusion.1, f32[256,8]{0,1:T(8,128)S(1)} %fusion.70), kind=kOutput, calls=%fused_computation.17 | convolution fusion | flops 51281920 | bytes 205824
  83.0 7.3 %all-to-all-start.2 = ((f32[32,1,512]{2,1,0:T(1,128)}), f32[32,1,512]{2,1,0:T(1,128)S(1)}, u32[]{:S(2)}, u32[]{:S(2)}) async-start(f32[32,1,512]{2,1,0:T(1,128)} %reshape.624), calls=%async_computation.2 | async-start | bytes 131072 | tf_op jit(solution)/shard_map/all_to_all | solution.py:80
  90.3 1.4 convolution_bitcast_fusion
  91.7 1.4 fusion.14
  94.7 8.2 %all-to-all-done.2 = f32[32,1,512]{2,1,0:T(1,128)S(1)} async-done(((f32[32,1,512]{2,1,0:T(1,128)}), f32[32,1,512]{2,1,0:T(1,128)S(1)}, u32[]{:S(2)}, u32[]{:S(2)}) %all-to-all-start.2) | async-done | bytes 65568 | tf_op jit(solution)/shard_map/all_to_all | solution.py:80
  102.9 4.3 %all-to-all-start.3 = ((f32[32,1,512]{2,1,0:T(1,128)}), f32[32,1,512]{2,1,0:T(1,128)S(1)}, u32[]{:S(2)}, u32[]{:S(2)}) async-start(f32[32,1,512]{2,1,0:T(1,128)} %reshape.626), calls=%async_computation.3 | async-start | bytes 131072 | tf_op jit(solution)/shard_map/all_to_all | solution.py:81
  108.6 1.7 copy.73
  110.4 2.2 copy.55
  114.4 5.5 %all-to-all-done.3 = f32[32,1,512]{2,1,0:T(1,128)S(1)} async-done(((f32[32,1,512]{2,1,0:T(1,128)}), f32[32,1,512]{2,1,0:T(1,128)S(1)}, u32[]{:S(2)}, u32[]{:S(2)}) %all-to-all-start.3) | async-done | bytes 65568 | tf_op jit(solution)/shard_map/all_to_all | solution.py:81
  121.3 1.7 copy.74
  123.0 2.2 copy.60
  127.1 3.7 %fusion.19 = f32[64]{0:T(128)S(1)} fusion(bf16[64,8,8,256]{3,2,1,0:T(8,128)(2,1)S(1)} %bitcast.145, f32[8,8,256,1]{2,1,0,3:T(8,128)S(1)} %bitcast.159), kind=kOutput, calls=%fused_computation.28 | convolution fusion | flops 12582976 | bytes 2162944 | tf_op jit(solution)/shard_map/sczyx,szyx->c/dot_general | solution.py:12
  130.8 103.3 %psum.7 = f32[64]{0:T(128)} all-reduce(f32[64]{0:T(128)S(1)} %fusion.19), channel_id=1, replica_groups=mesh['dp'=16,'slab'=32] {'dp','slab'}, use_global_device_ids=true, to_apply=%region_1.2 | all-reduce | flops 64 | bytes 512 | tf_op jit(solution)/shard_map/psum | solution.py:89
  (50 shorter events, 26.2 us)
Async XLA Ops:
  0.6 1.6 copy-start
  0.6 4.1 %copy-start.3 = (bf16[1,8,8,256]{3,2,1,0:T(8,128)(2,1)S(1)}, bf16[1,8,8,256]{3,2,1,0:T(8,128)(2,1)}, u32[]{:S(2)}) copy-start(bf16[1,8,8,256]{3,2,1,0:T(8,128)(2,1)} %param.7) | copy-start | bytes 98308
  4.7 20.0 %copy-start.2 = (s32[8,2]{0,1:T(2,128)S(1)}, s32[8,2]{0,1:T(2,128)}, u32[]{:S(2)}) copy-start(s32[8,2]{0,1:T(2,128)} %param.10) | copy-start | bytes 196
  7.6 35.2 %copy-start.1 = (s32[256,256]{1,0:T(8,128)S(1)}, s32[256,256]{1,0:T(8,128)}, u32[]{:S(2)}) copy-start(s32[256,256]{1,0:T(8,128)} %param.11) | copy-start | bytes 786436
  7.6 29.7 %all-to-all-start = ((f32[32,1,512]{2,1,0:T(1,128)}), f32[32,1,512]{2,1,0:T(1,128)S(1)}, u32[]{:S(2)}, u32[]{:S(2)}) async-start(f32[32,1,512]{2,1,0:T(1,128)} %reshape.620), calls=%async_computation | async-start | bytes 131072 | tf_op jit(solution)/shard_map/all_to_all | solution.py:56
  37.3 17.6 %all-to-all-start.1 = ((f32[32,1,512]{2,1,0:T(1,128)}), f32[32,1,512]{2,1,0:T(1,128)S(1)}, u32[]{:S(2)}, u32[]{:S(2)}) async-start(f32[32,1,512]{2,1,0:T(1,128)} %reshape.622), calls=%async_computation.1 | async-start | bytes 131072 | tf_op jit(solution)/shard_map/all_to_all | solution.py:57
  83.0 19.9 %all-to-all-start.2 = ((f32[32,1,512]{2,1,0:T(1,128)}), f32[32,1,512]{2,1,0:T(1,128)S(1)}, u32[]{:S(2)}, u32[]{:S(2)}) async-start(f32[32,1,512]{2,1,0:T(1,128)} %reshape.624), calls=%async_computation.2 | async-start | bytes 131072 | tf_op jit(solution)/shard_map/all_to_all | solution.py:80
  102.9 17.0 %all-to-all-start.3 = ((f32[32,1,512]{2,1,0:T(1,128)}), f32[32,1,512]{2,1,0:T(1,128)S(1)}, u32[]{:S(2)}, u32[]{:S(2)}) async-start(f32[32,1,512]{2,1,0:T(1,128)} %reshape.626), calls=%async_computation.3 | async-start | bytes 131072 | tf_op jit(solution)/shard_map/all_to_all | solution.py:81
  127.1 107.0 %copy-start.4 = (f32[8,8,256]{2,1,0:T(8,128)}, f32[8,8,256]{2,1,0:T(8,128)S(1)}, u32[]{:S(2)}) copy-start(f32[8,8,256]{2,1,0:T(8,128)S(1)} %fusion.15) | copy-start | bytes 196612
where the time goes:
time: 234 us
  blocking collectives  103 us (44%)
  matrix products  36.3 us (16%)
  starting transfers between devices  34 us (15%)
  local copies, waits for them, and re-layouts  28.9 us (12%)
  waiting for transfers between devices  26.4 us (11%)
  other arithmetic  3.4 us (1%)
    psum x1, blocking collectives, on_device(): w_grad = lax.psum(local_sum, ('dp', 'slab'))  103 us
    unnamed x8, matrix products  23.5 us
    all_to_all x1, starting transfers between devices, on_device(): lax.all_to_all(line_real, 'slab', split_axis=3, concat_axis=1, tiled=True)  17.1 us
    dot_general x6, matrix products, product(): return jnp.einsum(form, left, right, precision=lax.Precision.HIGHEST)  12.8 us
    unnamed x21, local copies, waits for them, and re-layouts  8.9 us
    all_to_all x1, waiting for transfers between devices, on_device(): lax.all_to_all(back_real, 'slab', split_axis=1, concat_axis=3, tiled=True)  8.22 us
    all_to_all x1, waiting for transfers between devices, on_device(): lax.all_to_all(line_real, 'slab', split_axis=3, concat_axis=1, tiled=True)  7.52 us
    all_to_all x1, starting transfers between devices, on_device(): lax.all_to_all(back_real, 'slab', split_axis=1, concat_axis=3, tiled=True)  7.34 us
  transfers between devices with their start and end apart: 4, of which 4 were waited for; matrix products, arithmetic and copies ran while one was open for 10% of the time, Pallas kernels for 0%

commit v1 on v0

v1 whole, which is shorter than its diff:
```python
import functools
import math

import jax
import jax.numpy as jnp
import numpy as np
from jax import lax
from jax.experimental import pallas as pl
from jax.experimental.pallas import tpu as pltpu
from jax.sharding import Mesh
from jax.sharding import PartitionSpec as P

N = 256
C = 64
BLK = 64
NB = 8
SLABS = 32
ZL = 8
YP = 8
ROWS = ZL * YP
CHUNKS = 4
PARTS = {"dp": (("y", 4), ("xh", 2), ("core", 2)), "slab": (("z", 16), ("xl", 2))}
NEAR = ("y", "xh")
FAR = ("core", "z", "xl")

F32, BF16 = jnp.float32, jnp.bfloat16
VMEM_LIMIT = 16 * 1024 * 1024


def halves(table):
    high = table.astype(np.float32).astype(BF16)
    low = (table - high.astype(np.float64)).astype(np.float32).astype(BF16)
    return high, low


def tables():
    step = 2.0 * math.pi / N
    space = np.arange(N)
    quad, slab = np.meshgrid(np.arange(4), np.arange(SLABS), indexing="ij")
    freq = (4 * slab + quad).reshape(-1)
    phase = (freq[:, None] * space[None, :]) % N * step
    real, imag = np.cos(phase), -np.sin(phase)
    imag[freq == 0] = np.cos(math.pi * space)
    forward = np.concatenate([real, imag], 0)
    weight = np.where(freq == 0, 1.0, 2.0)[:, None] / (N * N)
    inverse = np.concatenate([real * weight, imag * weight], 0)
    zp, m, i = np.meshgrid(np.arange(2), np.arange(4), np.arange(SLABS), indexing="ij")
    depth = (8 * i + 2 * m + zp).reshape(-1)
    phase = (space[:, None] * depth[None, :]) % N * step
    along = np.concatenate([np.cos(phase), np.sin(phase)], 0)
    return halves(forward), halves(along), halves(along.T.copy()), halves(inverse)


def split(values):
    high = values.astype(BF16)
    return high, (values - high.astype(F32)).astype(BF16)


def dot(left, right, dims=((1,), (0,))):
    return lax.dot_general(left, right, (dims, ((), ())), preferred_element_type=F32)


def lane_of(shape):
    return lax.broadcasted_iota(jnp.int32, shape, 1)


def regroup(pieces, to):
    group = (lane_of(pieces[0].shape) >> 4) & 3
    result = None
    for source in range(4):
        moved = pieces[source] if source == to else pltpu.roll(pieces[source], (16 * (source - to)) % 128, 1)
        result = moved if result is None else jnp.where(group == source, moved, result)
    return result


def filter_weights(turn, place, blocks, wedge, out):
    kz = lax.broadcasted_iota(jnp.int32, (8, N), 0)
    kx = lane_of((8, N)) >> 6
    listed = jnp.zeros((8, N), jnp.bool_)
    for n in range(NB):
        listed = listed | ((kz == blocks[n, 0]) & (kx == blocks[n, 1]))
    listed = listed.astype(F32)
    mask = jnp.concatenate(
        [wedge[a * BLK : (a + 1) * BLK, :].astype(F32) * listed[a : a + 1, :] for a in range(N // BLK)], 0
    ).astype(BF16)
    lane = lane_of((N, 128))
    row = lax.broadcasted_iota(jnp.int32, (N, 128), 0)
    quad = (lane >> 4) & 3
    freq = 4 * place + quad
    freq = jnp.where((freq == 0) & (lane >= 64), N // 2, freq)
    plus = (row == freq).astype(F32).astype(BF16)
    minus = (row == ((N - freq) & (N - 1))).astype(F32).astype(BF16)
    picks = jnp.concatenate([plus, minus], 1)
    odd = (turn & 1) == 1
    plain = dot(mask, picks)
    other = dot(mask, picks, ((0,), (0,)))
    direct = jnp.where(odd, other[:, 128:], plain[:, :128])
    mirror = jnp.where(odd, other[:, :128], plain[:, 128:]).astype(BF16)
    p = lax.broadcasted_iota(jnp.int32, (N, N), 0)
    s = lane_of((N, N))
    flip = (((p + s) & (N - 1)) == 0).astype(F32).astype(BF16)
    out[...] = direct + dot(flip, mirror)


def forward_x(place, turn, weight, blocks, wedge, features, target, fwd_high, fwd_low, lines, factors, held, sems):
    part = C * ROWS // CHUNKS
    copies = []
    for k in range(CHUNKS):
        rows = pl.ds(k * part, part)
        copies.append(pltpu.make_async_copy(features.at[rows], held.at[rows], sems.at[k]))
        copies[-1].start()
    filter_weights(turn[0], place[0], blocks, wedge, factors)
    total = -target[...].astype(F32)
    for k in range(CHUNKS):
        copies[k].wait()
        for c in range(k * C // CHUNKS, (k + 1) * C // CHUNKS):
            total = total + weight[c] * held[c * ROWS : (c + 1) * ROWS, :].astype(F32)
    high, low = split(total)
    high = jnp.concatenate([high, high], 0)
    low = jnp.concatenate([low, low], 0)
    nt = ((1,), (1,))
    line = dot(fwd_high[...], high, nt) + (dot(fwd_high[...], low, nt) + dot(fwd_low[...], high, nt))
    line = jnp.where(lane_of((128, 128)) < 64, line[:128], line[128:])
    pieces = [line[q * SLABS : (q + 1) * SLABS] for q in range(4)]
    for m in range(4):
        lines[pl.ds(m, SLABS, stride=4), :] = regroup(pieces, m)


def filter_z(place, lines, factors, fwd_high, fwd_low, inv_high, inv_low, back):
    even = jnp.concatenate([lines[pl.ds(m, SLABS, stride=4), :] for m in range(4)], 0)
    data = jnp.concatenate([even, pltpu.roll(even, 120, 1)], 0)
    high, low = split(data)
    freq = dot(fwd_high[...], high) + (dot(fwd_high[...], low) + dot(fwd_low[...], high))
    cosine, sine = freq[:N], freq[N:]
    lane = lane_of((N, 128))
    sign = jnp.where(lane < 64, 1.0, -1.0)
    sign = jnp.where((place[0] == 0) & (((lane >> 4) & 3) == 0), 0.0, sign)
    scale = factors[...]
    kept_cosine = scale * (cosine + sign * pltpu.roll(sine, 64, 1))
    kept_sine = scale * (sine - sign * pltpu.roll(cosine, 64, 1))
    high, low = split(jnp.concatenate([kept_cosine, kept_sine], 0))
    depth = dot(inv_high[...], high) + (dot(inv_high[...], low) + dot(inv_low[...], high))
    lane = lane_of((SLABS, 128))
    for m in range(4):
        first = depth[m * SLABS : (m + 1) * SLABS]
        second = depth[128 + m * SLABS : 128 + (m + 1) * SLABS]
        back[pl.ds(m, SLABS, stride=4), :] = jnp.where((lane & 8) == 0, first, pltpu.roll(second, 8, 1))


def inverse_x(lines, features, inv_high, inv_low, volume, sums, partial):
    blocks = [lines[pl.ds(m, SLABS, stride=4), :] for m in range(4)]
    line = jnp.concatenate([regroup(blocks, q) for q in range(4)], 0).T
    line = jnp.concatenate([line[:64], line[64:]], 1)
    high, low = split(line)
    result = dot(high, inv_high[...]) + (dot(low, inv_high[...]) + dot(high, inv_low[...]))
    volume[...] = result

    def channels(step, carry):
        for k in range(8):
            c = step * 8 + k
            piece = features[pl.ds(pl.multiple_of(c * ROWS, ROWS), ROWS), :].astype(F32) * result
            piece = sum(piece[z * YP : (z + 1) * YP] for z in range(ZL))
            partial[pl.ds(pl.multiple_of(c * YP, YP), YP), :] = piece[:, :128] + piece[:, 128:]
        return carry

    lax.fori_loop(0, C // 8, channels, 0)
    total = sum(partial[pl.ds(y, C, stride=YP), :] for y in range(YP))
    total = jnp.concatenate([total, jnp.zeros((128 - C, 128), F32)], 0)
    high, low = split(total)
    rest = (total - high.astype(F32) - low.astype(F32)).astype(BF16)
    ones = jnp.ones((sums.shape[0], 128), BF16)
    nt = ((1,), (1,))
    sums[...] = dot(ones, high, nt) + (dot(ones, low, nt) + dot(ones, rest, nt))


def call(body, outs, spaces, scratch=(), cost=(0, 0)):
    whole = {"v": pl.BlockSpec(memory_space=pltpu.VMEM), "s": pl.BlockSpec(memory_space=pltpu.SMEM), "a": pl.BlockSpec(memory_space=pl.ANY)}
    return pl.pallas_call(
        body,
        out_shape=[jax.ShapeDtypeStruct(shape, F32) for shape in outs],
        in_specs=[whole[space] for space in spaces],
        out_specs=[whole["v"] for _ in outs],
        scratch_shapes=list(scratch),
        compiler_params=pltpu.CompilerParams(vmem_limit_bytes=VMEM_LIMIT),
        cost_estimate=pl.CostEstimate(flops=cost[0], bytes_accessed=cost[1], transcendentals=0),
    )


def on_device(sizes, features, target, out_weight, rotation, blocks, wedge):
    fwd_x, fwd_z, inv_z, inv_x = tables()
    slab = tuple(name for name, _ in PARTS["slab"])
    place = lax.axis_index(slab).astype(jnp.int32).reshape(1)
    features = features.reshape(C * ROWS, N)
    target = target.reshape(ROWS, N)
    lines, factors = call(
        forward_x,
        [(128, 128), (N, 128)],
        "ssssvavvv",
        [pltpu.VMEM((C * ROWS, N), BF16), pltpu.SemaphoreType.DMA((CHUNKS,))],
        (200_000_000, 3_000_000),
    )(place, rotation, out_weight, blocks, wedge, features, target, *fwd_x)
    lines = lax.all_to_all(lines.reshape(SLABS, 4, 128), slab, 0, 0, tiled=True).reshape(128, 128)
    (back,) = call(filter_z, [(128, 128)], "svvvvvv", (), (200_000_000, 2_000_000))(place, lines, factors, *fwd_z, *inv_z)
    back = lax.all_to_all(back.reshape(SLABS, 4, 128), slab, 0, 0, tiled=True).reshape(128, 128)
    far = math.prod(sizes[name] for name in FAR)
    near = math.prod(sizes[name] for name in NEAR)
    volume, sums = call(
        inverse_x,
        [(ROWS, N), (far, 128)],
        "vvvv",
        [pltpu.VMEM((C * YP, 128), F32)],
        (200_000_000, 3_000_000),
    )(back, features, *inv_x)
    sums = lax.all_to_all(sums.reshape(far, 1, 128), FAR, 0, 0, tiled=True)
    sums = jnp.sum(sums, 0, keepdims=True)
    sums = jnp.broadcast_to(sums, (near, 1, 128))
    sums = lax.all_to_all(sums, NEAR, 0, 0, tiled=True)
    w_grad = jnp.sum(sums, (0, 1))[:C] * (1.0 / (math.prod(sizes.values()) * ROWS * N))
    return volume.reshape(1, ZL, YP, N), w_grad


def solution(mesh):
    parts = PARTS["dp"] + PARTS["slab"]
    sizes = dict(parts)
    dp = tuple(name for name, _ in PARTS["dp"])
    slab = tuple(name for name, _ in PARTS["slab"])
    fine = Mesh(mesh.devices.reshape([size for _, size in parts]), tuple(sizes))
    in_specs = (P(dp, None, slab, None, None), P(dp, slab, None, None), P(), P(dp), P(), P())
    out_specs = (P(dp, slab, None, None), P())
    return jax.shard_map(
        functools.partial(on_device, sizes), mesh=fine, in_specs=in_specs, out_specs=out_specs, check_vma=False
    )
```

time: 234 us -> 93.8 us (0.40)
  matrix products: 36.3 us -> 0 us
  starting transfers between devices: 34 us -> 0 us
  waiting for transfers between devices: 26.4 us -> 0 us
  blocking collectives: 103 us -> 77.1 us
  local copies, waits for them, and re-layouts: 28.9 us -> 9.34 us
  Pallas kernels: 0 us -> 4.86 us
  other arithmetic: 3.4 us -> 0.62 us
    psum x1 -> x0, blocking collectives: 103 us -> none  [on_device(): w_grad = lax.psum(local_sum, ('dp', 'slab'))]
    all_to_all x0 -> x4, blocking collectives: none -> 77.1 us  [the longest x1 29.4 us: on_device(): lax.all_to_all(lines.reshape(SLABS, 4, 128), slab, 0, 0, tiled=True)]
    all_to_all x4 -> x0, starting transfers between devices: 34 us -> none  [the longest x1 17.1 us: on_device(): lax.all_to_all(line_real, 'slab', split_axis=3, concat_axis=1, tiled=True)]
    all_to_all x4 -> x0, waiting for transfers between devices: 26.4 us -> none  [the longest x1 8.22 us: on_device(): lax.all_to_all(back_real, 'slab', split_axis=1, concat_axis=3, tiled=True)]
    unnamed x8 -> x0, matrix products: 23.5 us -> none
    all_to_all x9 -> x0, local copies, waits for them, and re-layouts: 16.1 us -> none  [the longest x3 4.4 us: on_device(): lax.all_to_all(line_real, 'slab', split_axis=3, concat_axis=1, tiled=True)]
    dot_general x6 -> x0, matrix products: 12.8 us -> none  [product(): return jnp.einsum(form, left, right, precision=lax.Precision.HIGHEST)]
    pallas_call x0 -> x3, Pallas kernels: none -> 4.86 us  [the longest x1 2.14 us: on_device(): call(forward_x, [(128, 128), (N, 128)], 'ssssvavvv', [pltpu.VMEM((C * ROW...]
  transfers between devices with their start and end apart: 4 -> 0, of which waited for: 4 -> 0; matrix products, arithmetic and copies ran while one was open for 10% -> 0% of each run, Pallas kernels for 0% -> 0%
where the time goes in v1:
time: 93.8 us; the launch traced here: 93.3 us
  blocking collectives  77.1 us (82%)
  local copies, waits for them, and re-layouts  9.34 us (10%)
  Pallas kernels  4.86 us (5%)
  between operations  1.32 us (1%)
    all_to_all x1, blocking collectives, on_device(): lax.all_to_all(lines.reshape(SLABS, 4, 128), slab, 0, 0, tiled=True)  29.4 us
    all_to_all x1, blocking collectives, on_device(): sums = lax.all_to_all(sums.reshape(far, 1, 128), FAR, 0, 0, tiled=True)  19.6 us
    all_to_all x1, blocking collectives, on_device(): lax.all_to_all(back.reshape(SLABS, 4, 128), slab, 0, 0, tiled=True)  15.5 us
    all_to_all x1, blocking collectives, on_device(): sums = lax.all_to_all(sums, NEAR, 0, 0, tiled=True)  12.7 us
    unnamed x27, local copies, waits for them, and re-layouts  9.33 us
    pallas_call x1, Pallas kernels, on_device(): call(forward_x, [(128, 128), (N, 128)], 'ssssvavvv', [pltpu.VMEM((C * ROW...  2.14 us

profile of v1, /device:TPU:1, one launch (start us, length us, event | category | flops | bytes accessed | tf_op | source)
XLA Modules:
  0.0 93.3 jit_solution(10342379206196452881)
XLA Ops:
  1.3 0.8 copy.21.blocks
  2.0 1.6 %copy-done = bf16[1,64,8,8,256]{4,3,2,1,0:T(8,128)(2,1)S(1)} copy-done((bf16[1,64,8,8,256]{4,3,2,1,0:T(8,128)(2,1)S(1)}, bf16[1,64,8,8,256]{4,3,2,1,0:T(8,128)(2,1)}, u32[]{:S(2)}) %copy-start) | copy-done | bytes 2097176
  3.6 0.0 copy-start.6
  3.6 0.9 %copy-done.6 = s32[256,256]{1,0:T(8,128)S(1)} copy-done((s32[256,256]{1,0:T(8,128)S(1)}, s32[256,256]{1,0:T(8,128)}, u32[]{:S(2)}) %copy-start.6) | copy-done | bytes 262168
  4.6 0.9 copy-done.9
  5.5 0.9 copy-done.10
  6.4 0.8 copy-done.11
  7.1 0.7 copy-done.12
  7.8 2.1 %shard_map.149 = (f32[128,128]{1,0:T(8,128)S(1)}, f32[256,128]{1,0:T(8,128)S(1)}) custom-call(s32[1]{0:T(128)} %bitcast.place, s32[1]{0:T(128)S(6)} %copy.24.turn, f32[64]{0:T(128)S(1)} %copy-done.12, s32[8,2]{1,0:T(8,128)S(1)} %copy.21.blocks, s32[256,256]{1,0:T(8,128)S(1)} %copy-done.6, bf16[4096,256]{1,0:T(8,128)(2,1)S(1)} %bitcast.12, ...), custom_call_target="tpu_custom_call" | custom-call | flops 200000000 | bytes 3000000 | tf_op jit(solution)/shard_map/pallas_call | solution.py:195
  10.0 29.4 %all_to_all.20 = f32[32,4,128]{2,1,0:T(4,128)S(1)} all-to-all(f32[32,4,128]{2,1,0:T(4,128)S(1)} %bitcast.17), channel_id=1, replica_groups=mesh['y'=4,'xh'=2,'core'=2,'z'=16,'xl'=2] {'z','xl'}, dimensions={0} | all-to-all | bytes 131072 | tf_op jit(solution)/shard_map/all_to_all | solution.py:202
  39.3 0.0 copy-done.2
  39.4 0.0 copy-done.3
  39.4 0.9 %copy-done.4 = bf16[512,256]{1,0:T(8,128)(2,1)S(1)} copy-done((bf16[512,256]{1,0:T(8,128)(2,1)S(1)}, bf16[512,256]{1,0:T(8,128)(2,1)}, u32[]{:S(2)}) %copy-start.4) | copy-done | bytes 262168
  40.3 0.9 %copy-done.5 = bf16[512,256]{1,0:T(8,128)(2,1)S(1)} copy-done((bf16[512,256]{1,0:T(8,128)(2,1)S(1)}, bf16[512,256]{1,0:T(8,128)(2,1)}, u32[]{:S(2)}) %copy-start.5) | copy-done | bytes 262168
  41.3 1.3 %shard_map.150 = f32[128,128]{1,0:T(8,128)S(1)} custom-call(s32[1]{0:T(128)} %bitcast.place, f32[128,128]{1,0:T(8,128)S(1)} %bitcast.14, f32[256,128]{1,0:T(8,128)S(1)} %get-tuple-element.7.factors, bf16[512,256]{1,0:T(8,128)(2,1)S(1)} %copy-done.5, bf16[512,256]{1,0:T(8,128)(2,1)S(1)} %copy-done.4, bf16[256,512]{1,0:T(8,128)(2,1)S(1)} %copy-done.3, ...), custom_call_target="tpu_custom_call" | custom-call | flops 200000000 | bytes 2000000 | tf_op jit(solution)/shard_map/pallas_call | solution.py:203
  42.5 15.5 %all_to_all.21 = f32[32,4,128]{2,1,0:T(4,128)S(1)} all-to-all(f32[32,4,128]{2,1,0:T(4,128)S(1)} %bitcast.15), channel_id=1, replica_groups=mesh['y'=4,'xh'=2,'core'=2,'z'=16,'xl'=2] {'z','xl'}, dimensions={0} | all-to-all | bytes 131072 | tf_op jit(solution)/shard_map/all_to_all | solution.py:204
  58.0 0.0 copy-done.1
  58.0 0.0 copy-done.7
  58.0 0.9 copy-done.8
  58.9 1.5 %shard_map.151 = (f32[64,256]{1,0:T(8,128)}, f32[64,128]{1,0:T(8,128)S(1)}) custom-call(f32[128,128]{1,0:T(8,128)S(1)} %bitcast.16, bf16[4096,256]{1,0:T(8,128)(2,1)S(1)} %bitcast.13, bf16[256,256]{1,0:T(8,128)(2,1)S(1)} %copy-done.8, bf16[256,256]{1,0:T(8,128)(2,1)S(1)} %copy-done.7), custom_call_target="tpu_custom_call" | custom-call | flops 200000000 | bytes 3000000 | tf_op jit(solution)/shard_map/pallas_call | solution.py:207
  60.4 19.6 %all_to_all.22 = f32[64,1,128]{2,1,0:T(1,128)S(1)} all-to-all(f32[64,1,128]{2,1,0:T(1,128)S(1)} %bitcast.19), channel_id=1, replica_groups=mesh['y'=4,'xh'=2,'core'=2,'z'=16,'xl'=2] {'core','z','xl'}, dimensions={0} | all-to-all | bytes 65536 | tf_op jit(solution)/shard_map/all_to_all | solution.py:214
  80.0 0.1 reduce_sum.18
  80.1 12.7 %all_to_all.23 = f32[8,1,128]{2,1,0:T(1,128)S(1)} all-to-all(f32[8,1,128]{2,1,0:T(1,128)S(1)} %broadcast_in_dim.2), channel_id=1, replica_groups=mesh['y'=4,'xh'=2,'core'=2,'z'=16,'xl'=2] {'y','xh'}, dimensions={0} | all-to-all | bytes 8192 | tf_op jit(solution)/shard_map/all_to_all | solution.py:217
  92.7 0.5 slice_multiply_fusion
  (14 shorter events, 0.0 us)
Async XLA Ops:
  2.0 1.6 %copy-start = (bf16[1,64,8,8,256]{4,3,2,1,0:T(8,128)(2,1)S(1)}, bf16[1,64,8,8,256]{4,3,2,1,0:T(8,128)(2,1)}, u32[]{:S(2)}) copy-start(bf16[1,64,8,8,256]{4,3,2,1,0:T(8,128)(2,1)} %param.14) | copy-start | bytes 6291460
  3.6 0.9 %copy-start.6 = (s32[256,256]{1,0:T(8,128)S(1)}, s32[256,256]{1,0:T(8,128)}, u32[]{:S(2)}) copy-start(s32[256,256]{1,0:T(8,128)} %wedge.1) | copy-start | bytes 786436
  4.6 0.9 copy-start.9
  5.5 0.9 copy-start.10
  6.4 0.8 copy-start.11
  7.1 0.7 copy-start.12
  7.8 31.5 %copy-start.2 = (bf16[256,512]{1,0:T(8,128)(2,1)S(1)}, bf16[256,512]{1,0:T(8,128)(2,1)}, u32[]{:S(2)}) copy-start(bf16[256,512]{1,0:T(8,128)(2,1)} %constant.35.clone.inv_low) | copy-start | bytes 786436
  7.8 31.6 %copy-start.3 = (bf16[256,512]{1,0:T(8,128)(2,1)S(1)}, bf16[256,512]{1,0:T(8,128)(2,1)}, u32[]{:S(2)}) copy-start(bf16[256,512]{1,0:T(8,128)(2,1)} %constant.34.clone.inv_high) | copy-start | bytes 786436
  7.8 50.2 %copy-start.1 = (bf16[1,64,8,8,256]{4,3,2,1,0:T(8,128)(2,1)S(1)}, bf16[1,64,8,8,256]{4,3,2,1,0:T(8,128)(2,1)}, u32[]{:S(2)}) copy-start(bf16[1,64,8,8,256]{4,3,2,1,0:T(8,128)(2,1)} %param.14) | copy-start | bytes 6291460
  7.8 50.2 %copy-start.7 = (bf16[256,256]{1,0:T(8,128)(2,1)S(1)}, bf16[256,256]{1,0:T(8,128)(2,1)}, u32[]{:S(2)}) copy-start(bf16[256,256]{1,0:T(8,128)(2,1)} %constant.37.clone.inv_low) | copy-start | bytes 393220
  39.4 1.0 %copy-start.4 = (bf16[512,256]{1,0:T(8,128)(2,1)S(1)}, bf16[512,256]{1,0:T(8,128)(2,1)}, u32[]{:S(2)}) copy-start(bf16[512,256]{1,0:T(8,128)(2,1)} %constant.33.clone.fwd_low) | copy-start | bytes 786436
  40.3 0.9 %copy-start.5 = (bf16[512,256]{1,0:T(8,128)(2,1)S(1)}, bf16[512,256]{1,0:T(8,128)(2,1)}, u32[]{:S(2)}) copy-start(bf16[512,256]{1,0:T(8,128)(2,1)} %constant.32.clone.fwd_high) | copy-start | bytes 786436
  58.0 0.9 copy-start.8

commit v2 on v1

--- a/solution.py
+++ b/solution.py
@@ -41,14 +41,11 @@
     phase = (freq[:, None] * space[None, :]) % N * step
     real, imag = np.cos(phase), -np.sin(phase)
     imag[freq == 0] = np.cos(math.pi * space)
-    forward = np.concatenate([real, imag], 0)
-    weight = np.where(freq == 0, 1.0, 2.0)[:, None] / (N * N)
-    inverse = np.concatenate([real * weight, imag * weight], 0)
     zp, m, i = np.meshgrid(np.arange(2), np.arange(4), np.arange(SLABS), indexing="ij")
     depth = (8 * i + 2 * m + zp).reshape(-1)
-    phase = (space[:, None] * depth[None, :]) % N * step
+    phase = (depth[:, None] * depth[None, :]) % N * step
     along = np.concatenate([np.cos(phase), np.sin(phase)], 0)
-    return halves(forward), halves(along), halves(along.T.copy()), halves(inverse)
+    return halves(np.concatenate([real, imag], 0)) + halves(along)
 
 
 def split(values):
@@ -78,7 +75,7 @@
     kx = lane_of((8, N)) >> 6
     listed = jnp.zeros((8, N), jnp.bool_)
     for n in range(NB):
-        listed = listed | ((kz == blocks[n, 0]) & (kx == blocks[n, 1]))
+        listed = listed | ((kz == blocks[0, n]) & (kx == blocks[1, n]))
     listed = listed.astype(F32)
     mask = jnp.concatenate(
         [wedge[a * BLK : (a + 1) * BLK, :].astype(F32) * listed[a : a + 1, :] for a in range(N // BLK)], 0
@@ -96,29 +93,45 @@
     other = dot(mask, picks, ((0,), (0,)))
     direct = jnp.where(odd, other[:, 128:], plain[:, :128])
     mirror = jnp.where(odd, other[:, :128], plain[:, 128:]).astype(BF16)
-    p = lax.broadcasted_iota(jnp.int32, (N, N), 0)
-    s = lane_of((N, N))
-    flip = (((p + s) & (N - 1)) == 0).astype(F32).astype(BF16)
-    out[...] = direct + dot(flip, mirror)
-
-
-def forward_x(place, turn, weight, blocks, wedge, features, target, fwd_high, fwd_low, lines, factors, held, sems):
+    r = lax.broadcasted_iota(jnp.int32, (N, N), 0)
+    p = 8 * (r & 31) + 2 * ((r >> 5) & 3) + (r >> 7)
+    k = lane_of((N, N))
+    keep = (k == p).astype(F32).astype(BF16)
+    flip = (((p + k) & (N - 1)) == 0).astype(F32).astype(BF16)
+    out[...] = dot(keep, direct.astype(BF16)) + dot(flip, mirror)
+
+
+def forward_x(
+    place, turn, weight_hbm, blocks_hbm, wedge_hbm, features_hbm, target_hbm, *refs
+):
+    tables_hbm, (lines, factors, features), held = refs[:4], refs[4:7], refs[7:11]
+    weight, blocks, wedge, target, sems = refs[11:]
     part = C * ROWS // CHUNKS
-    copies = []
+    pairs = [(weight_hbm, weight), (blocks_hbm, blocks), (wedge_hbm, wedge), (target_hbm, target)]
     for k in range(CHUNKS):
         rows = pl.ds(k * part, part)
-        copies.append(pltpu.make_async_copy(features.at[rows], held.at[rows], sems.at[k]))
-        copies[-1].start()
+        pairs.append((features_hbm.at[rows], features.at[rows]))
+    pairs += list(zip(tables_hbm, held))
+    copies = [pltpu.make_async_copy(source, goal, sems.at[n]) for n, (source, goal) in enumerate(pairs)]
+    for copy in copies:
+        copy.start()
+    for copy in copies[1:3]:
+        copy.wait()
     filter_weights(turn[0], place[0], blocks, wedge, factors)
+    copies[0].wait()
+    copies[3].wait()
     total = -target[...].astype(F32)
     for k in range(CHUNKS):
-        copies[k].wait()
+        copies[4 + k].wait()
         for c in range(k * C // CHUNKS, (k + 1) * C // CHUNKS):
-            total = total + weight[c] * held[c * ROWS : (c + 1) * ROWS, :].astype(F32)
+            total = total + weight[c] * features[c * ROWS : (c + 1) * ROWS, :].astype(F32)
     high, low = split(total)
     high = jnp.concatenate([high, high], 0)
     low = jnp.concatenate([low, low], 0)
     nt = ((1,), (1,))
+    for copy in copies[4 + CHUNKS :]:
+        copy.wait()
+    fwd_high, fwd_low = held[:2]
     line = dot(fwd_high[...], high, nt) + (dot(fwd_high[...], low, nt) + dot(fwd_low[...], high, nt))
     line = jnp.where(lane_of((128, 128)) < 64, line[:128], line[128:])
     pieces = [line[q * SLABS : (q + 1) * SLABS] for q in range(4)]
@@ -126,11 +139,11 @@
         lines[pl.ds(m, SLABS, stride=4), :] = regroup(pieces, m)
 
 
-def filter_z(place, lines, factors, fwd_high, fwd_low, inv_high, inv_low, back):
+def filter_z(place, lines, factors, along_high, along_low, back):
     even = jnp.concatenate([lines[pl.ds(m, SLABS, stride=4), :] for m in range(4)], 0)
     data = jnp.concatenate([even, pltpu.roll(even, 120, 1)], 0)
     high, low = split(data)
-    freq = dot(fwd_high[...], high) + (dot(fwd_high[...], low) + dot(fwd_low[...], high))
+    freq = dot(along_high[...], high) + (dot(along_high[...], low) + dot(along_low[...], high))
     cosine, sine = freq[:N], freq[N:]
     lane = lane_of((N, 128))
     sign = jnp.where(lane < 64, 1.0, -1.0)
@@ -138,8 +151,11 @@
     scale = factors[...]
     kept_cosine = scale * (cosine + sign * pltpu.roll(sine, 64, 1))
     kept_sine = scale * (sine - sign * pltpu.roll(cosine, 64, 1))
-    high, low = split(jnp.concatenate([kept_cosine, kept_sine], 0))
-    depth = dot(inv_high[...], high) + (dot(inv_high[...], low) + dot(inv_low[...], high))
+    depth = None
+    for kept, rows in ((kept_cosine, slice(0, N)), (kept_sine, slice(N, 2 * N))):
+        high, low = split(kept)
+        term = dot(along_high[rows, :], high) + (dot(along_high[rows, :], low) + dot(along_low[rows, :], high))
+        depth = term if depth is None else depth + term
     lane = lane_of((SLABS, 128))
     for m in range(4):
         first = depth[m * SLABS : (m + 1) * SLABS]
@@ -147,18 +163,21 @@
         back[pl.ds(m, SLABS, stride=4), :] = jnp.where((lane & 8) == 0, first, pltpu.roll(second, 8, 1))
 
 
-def inverse_x(lines, features, inv_high, inv_low, volume, sums, partial):
+def inverse_x(lines, features, fwd_high, fwd_low, volume, sums, result, partial, sem):
     blocks = [lines[pl.ds(m, SLABS, stride=4), :] for m in range(4)]
     line = jnp.concatenate([regroup(blocks, q) for q in range(4)], 0).T
     line = jnp.concatenate([line[:64], line[64:]], 1)
+    line = line * jnp.where((lane_of((ROWS, N)) & 127) == 0, 1.0 / (N * N), 2.0 / (N * N))
     high, low = split(line)
-    result = dot(high, inv_high[...]) + (dot(low, inv_high[...]) + dot(high, inv_low[...]))
-    volume[...] = result
+    values = dot(high, fwd_high[...]) + (dot(low, fwd_high[...]) + dot(high, fwd_low[...]))
+    result[...] = values
+    leave = pltpu.make_async_copy(result, volume, sem)
+    leave.start()
 
     def channels(step, carry):
         for k in range(8):
             c = step * 8 + k
-            piece = features[pl.ds(pl.multiple_of(c * ROWS, ROWS), ROWS), :].astype(F32) * result
+            piece = features[pl.ds(pl.multiple_of(c * ROWS, ROWS), ROWS), :].astype(F32) * values
             piece = sum(piece[z * YP : (z + 1) * YP] for z in range(ZL))
             partial[pl.ds(pl.multiple_of(c * YP, YP), YP), :] = piece[:, :128] + piece[:, 128:]
         return carry
@@ -171,15 +190,17 @@
     ones = jnp.ones((sums.shape[0], 128), BF16)
     nt = ((1,), (1,))
     sums[...] = dot(ones, high, nt) + (dot(ones, low, nt) + dot(ones, rest, nt))
+    leave.wait()
 
 
 def call(body, outs, spaces, scratch=(), cost=(0, 0)):
-    whole = {"v": pl.BlockSpec(memory_space=pltpu.VMEM), "s": pl.BlockSpec(memory_space=pltpu.SMEM), "a": pl.BlockSpec(memory_space=pl.ANY)}
+    whole = {"v": pl.BlockSpec(memory_space=pltpu.VMEM), "s": pl.BlockSpec(memory_space=pltpu.SMEM), "h": pl.BlockSpec(memory_space=pltpu.HBM)}
+    ins, goals = spaces.split(">")
     return pl.pallas_call(
         body,
-        out_shape=[jax.ShapeDtypeStruct(shape, F32) for shape in outs],
-        in_specs=[whole[space] for space in spaces],
-        out_specs=[whole["v"] for _ in outs],
+        out_shape=[jax.ShapeDtypeStruct(shape, kind) for shape, kind in outs],
+        in_specs=[whole[space] for space in ins],
+        out_specs=[whole[space] for space in goals],
         scratch_shapes=list(scratch),
         compiler_params=pltpu.CompilerParams(vmem_limit_bytes=VMEM_LIMIT),
         cost_estimate=pl.CostEstimate(flops=cost[0], bytes_accessed=cost[1], transcendentals=0),
@@ -187,30 +208,41 @@
 
 
 def on_device(sizes, features, target, out_weight, rotation, blocks, wedge):
-    fwd_x, fwd_z, inv_z, inv_x = tables()
     slab = tuple(name for name, _ in PARTS["slab"])
     place = lax.axis_index(slab).astype(jnp.int32).reshape(1)
     features = features.reshape(C * ROWS, N)
     target = target.reshape(ROWS, N)
-    lines, factors = call(
+    inputs = [
+        pltpu.with_memory_space_constraint(jnp.asarray(each), pltpu.HBM)
+        for each in (out_weight, blocks.T, wedge, features, target) + tables()
+    ]
+    lines, factors, features, fwd_high, fwd_low, along_high, along_low = call(
         forward_x,
-        [(128, 128), (N, 128)],
-        "ssssvavvv",
-        [pltpu.VMEM((C * ROWS, N), BF16), pltpu.SemaphoreType.DMA((CHUNKS,))],
+        [((128, 128), F32), ((N, 128), F32), ((C * ROWS, N), BF16)] + [(table.shape, BF16) for table in inputs[5:]],
+        "ss" + "h" * 9 + ">" + "v" * 7,
+        [
+            pltpu.SMEM((C,), F32),
+            pltpu.SMEM((2, NB), jnp.int32),
+            pltpu.VMEM((N, N), jnp.int32),
+            pltpu.VMEM((ROWS, N), BF16),
+            pltpu.SemaphoreType.DMA((8 + CHUNKS,)),
+        ],
         (200_000_000, 3_000_000),
-    )(place, rotation, out_weight, blocks, wedge, features, target, *fwd_x)
+    )(place, rotation, *inputs)
     lines = lax.all_to_all(lines.reshape(SLABS, 4, 128), slab, 0, 0, tiled=True).reshape(128, 128)
-    (back,) = call(filter_z, [(128, 128)], "svvvvvv", (), (200_000_000, 2_000_000))(place, lines, factors, *fwd_z, *inv_z)
+    (back,) = call(filter_z, [((128, 128), F32)], "svvvv>v", (), (200_000_000, 2_000_000))(
+        place, lines, factors, along_high, along_low
+    )
     back = lax.all_to_all(back.reshape(SLABS, 4, 128), slab, 0, 0, tiled=True).reshape(128, 128)
     far = math.prod(sizes[name] for name in FAR)
     near = math.prod(sizes[name] for name in NEAR)
     volume, sums = call(
         inverse_x,
-        [(ROWS, N), (far, 128)],
-        "vvvv",
-        [pltpu.VMEM((C * YP, 128), F32)],
+        [((ROWS, N), F32), ((far, 128), F32)],
+        "vvvv>hv",
+        [pltpu.VMEM((ROWS, N), F32), pltpu.VMEM((C * YP, 128), F32), pltpu.SemaphoreType.DMA],
         (200_000_000, 3_000_000),
-    )(back, features, *inv_x)
+    )(back, features, fwd_high, fwd_low)
     sums = lax.all_to_all(sums.reshape(far, 1, 128), FAR, 0, 0, tiled=True)
     sums = jnp.sum(sums, 0, keepdims=True)
     sums = jnp.broadcast_to(sums, (near, 1, 128))

time: 93.8 us -> 84.1 us (0.90)
  local copies, waits for them, and re-layouts: 9.34 us -> 0.01 us
    unnamed x27 -> x0, local copies, waits for them, and re-layouts: 9.33 us -> none
where the time goes in v2:
time: 84.1 us; the launch traced here: 83.9 us
  blocking collectives  77.1 us (92%)
  Pallas kernels  4.83 us (6%)
  between operations  1.31 us (2%)
    all_to_all x1, blocking collectives, on_device(): lax.all_to_all(lines.reshape(SLABS, 4, 128), slab, 0, 0, tiled=True)  29.4 us
    all_to_all x1, blocking collectives, on_device(): sums = lax.all_to_all(sums.reshape(far, 1, 128), FAR, 0, 0, tiled=True)  19.6 us
    all_to_all x1, blocking collectives, on_device(): lax.all_to_all(back.reshape(SLABS, 4, 128), slab, 0, 0, tiled=True)  15.5 us
    all_to_all x1, blocking collectives, on_device(): sums = lax.all_to_all(sums, NEAR, 0, 0, tiled=True)  12.7 us
    pallas_call x1, Pallas kernels, on_device(): call(forward_x, [((128, 128), F32), ((N, 128), F32), ((C * ROWS, N), BF16...  2.49 us

profile of v2, /device:TPU:1, one launch (start us, length us, event | category | flops | bytes accessed | tf_op | source)
XLA Modules:
  0.0 83.9 jit_solution(786881410341478253)
XLA Ops:
  1.3 2.5 %shard_map.113 = (f32[128,128]{1,0:T(8,128)S(1)}, f32[256,128]{1,0:T(8,128)S(1)}, bf16[4096,256]{1,0:T(8,128)(2,1)S(1)}, bf16[256,256]{1,0:T(8,128)(2,1)S(1)}, b...) custom-call(s32[1]{0:T(128)} %bitcast.place, s32[1]{0:T(128)S(6)} %copy.16.turn, ...), custom_call_target="tpu_custom_call" | custom-call | flops 200000000 | bytes 3000000 | tf_op jit(solution)/shard_map/pallas_call | solution.py:219
  3.8 29.4 %all_to_all.20 = f32[32,4,128]{2,1,0:T(4,128)S(1)} all-to-all(f32[32,4,128]{2,1,0:T(4,128)S(1)} %bitcast.16), channel_id=1, replica_groups=mesh['y'=4,'xh'=2,'core'=2,'z'=16,'xl'=2] {'z','xl'}, dimensions={0} | all-to-all | bytes 131072 | tf_op jit(solution)/shard_map/all_to_all | solution.py:232
  33.2 1.3 %shard_map.114 = f32[128,128]{1,0:T(8,128)S(1)} custom-call(s32[1]{0:T(128)} %bitcast.place, f32[128,128]{1,0:T(8,128)S(1)} %bitcast.14, f32[256,128]{1,0:T(8,128)S(1)} %get-tuple-element.12.factors, bf16[512,256]{1,0:T(8,128)(2,1)S(1)} %get-tuple-element.13.along_high, bf16[512,256]{1,0:T(8,128)(2,1)S(1)} %get-tuple-element.14.along_low), custom_call_target="tpu_custom_call" | custom-call | flops 200000000 | bytes 2000000 | tf_op jit(solution)/shard_map/pallas_call | solution.py:233
  34.4 15.5 %all_to_all.21 = f32[32,4,128]{2,1,0:T(4,128)S(1)} all-to-all(f32[32,4,128]{2,1,0:T(4,128)S(1)} %bitcast.15), channel_id=1, replica_groups=mesh['y'=4,'xh'=2,'core'=2,'z'=16,'xl'=2] {'z','xl'}, dimensions={0} | all-to-all | bytes 131072 | tf_op jit(solution)/shard_map/all_to_all | solution.py:236
  49.9 1.1 %shard_map.115 = (f32[64,256]{1,0:T(8,128)}, f32[64,128]{1,0:T(8,128)S(1)}) custom-call(f32[128,128]{1,0:T(8,128)S(1)} %bitcast.13, bf16[4096,256]{1,0:T(8,128)(2,1)S(1)} %get-tuple-element.15.features, bf16[256,256]{1,0:T(8,128)(2,1)S(1)} %get-tuple-element.16.fwd_high, bf16[256,256]{1,0:T(8,128)(2,1)S(1)} %get-tuple-element.17.fwd_low), custom_call_target="tpu_custom_call" | custom-call | flops 200000000 | bytes 3000000 | tf_op jit(solution)/shard_map/pallas_call | solution.py:239
  51.0 19.6 %all_to_all.22 = f32[64,1,128]{2,1,0:T(1,128)S(1)} all-to-all(f32[64,1,128]{2,1,0:T(1,128)S(1)} %bitcast.17), channel_id=1, replica_groups=mesh['y'=4,'xh'=2,'core'=2,'z'=16,'xl'=2] {'core','z','xl'}, dimensions={0} | all-to-all | bytes 65536 | tf_op jit(solution)/shard_map/all_to_all | solution.py:246
  70.6 0.1 reduce_sum.18
  70.7 12.7 %all_to_all.23 = f32[8,1,128]{2,1,0:T(1,128)S(1)} all-to-all(f32[8,1,128]{2,1,0:T(1,128)S(1)} %broadcast_in_dim.2), channel_id=1, replica_groups=mesh['y'=4,'xh'=2,'core'=2,'z'=16,'xl'=2] {'y','xh'}, dimensions={0} | all-to-all | bytes 8192 | tf_op jit(solution)/shard_map/all_to_all | solution.py:249
  83.4 0.5 slice_multiply_fusion
  (2 shorter events, 0.0 us)

commit v3 on v2

--- a/solution.py
+++ b/solution.py
@@ -68,6 +68,10 @@
         moved = pieces[source] if source == to else pltpu.roll(pieces[source], (16 * (source - to)) % 128, 1)
         result = moved if result is None else jnp.where(group == source, moved, result)
     return result
+
+
+def slab_index():
+    return lax.axis_index(tuple(name for name, _ in PARTS["slab"])).astype(jnp.int32)
 
 
 def filter_weights(turn, place, blocks, wedge, out):
@@ -102,12 +106,13 @@
 
 
 def forward_x(
-    place, turn, weight_hbm, blocks_hbm, wedge_hbm, features_hbm, target_hbm, *refs
+    turn, weight_hbm, blocks_hbm, wedge_hbm, features_hbm, target_hbm, *refs
 ):
     tables_hbm, (lines, factors, features), held = refs[:4], refs[4:7], refs[7:11]
     weight, blocks, wedge, target, sems = refs[11:]
     part = C * ROWS // CHUNKS
-    pairs = [(weight_hbm, weight), (blocks_hbm, blocks), (wedge_hbm, wedge), (target_hbm, target)]
+    small = [(blocks_hbm, blocks), (wedge_hbm, wedge), (weight_hbm, weight), (target_hbm, target)]
+    pairs = list(small)
     for k in range(CHUNKS):
         rows = pl.ds(k * part, part)
         pairs.append((features_hbm.at[rows], features.at[rows]))
@@ -115,21 +120,21 @@
     copies = [pltpu.make_async_copy(source, goal, sems.at[n]) for n, (source, goal) in enumerate(pairs)]
     for copy in copies:
         copy.start()
-    for copy in copies[1:3]:
+    for copy in copies[:2]:
         copy.wait()
-    filter_weights(turn[0], place[0], blocks, wedge, factors)
-    copies[0].wait()
-    copies[3].wait()
+    filter_weights(turn[0], slab_index(), blocks, wedge, factors)
+    for copy in copies[2 : len(small)]:
+        copy.wait()
     total = -target[...].astype(F32)
     for k in range(CHUNKS):
-        copies[4 + k].wait()
+        copies[len(small) + k].wait()
         for c in range(k * C // CHUNKS, (k + 1) * C // CHUNKS):
             total = total + weight[c] * features[c * ROWS : (c + 1) * ROWS, :].astype(F32)
     high, low = split(total)
     high = jnp.concatenate([high, high], 0)
     low = jnp.concatenate([low, low], 0)
     nt = ((1,), (1,))
-    for copy in copies[4 + CHUNKS :]:
+    for copy in copies[len(small) + CHUNKS :]:
         copy.wait()
     fwd_high, fwd_low = held[:2]
     line = dot(fwd_high[...], high, nt) + (dot(fwd_high[...], low, nt) + dot(fwd_low[...], high, nt))
@@ -139,7 +144,7 @@
         lines[pl.ds(m, SLABS, stride=4), :] = regroup(pieces, m)
 
 
-def filter_z(place, lines, factors, along_high, along_low, back):
+def filter_z(lines, factors, along_high, along_low, back):
     even = jnp.concatenate([lines[pl.ds(m, SLABS, stride=4), :] for m in range(4)], 0)
     data = jnp.concatenate([even, pltpu.roll(even, 120, 1)], 0)
     high, low = split(data)
@@ -147,7 +152,7 @@
     cosine, sine = freq[:N], freq[N:]
     lane = lane_of((N, 128))
     sign = jnp.where(lane < 64, 1.0, -1.0)
-    sign = jnp.where((place[0] == 0) & (((lane >> 4) & 3) == 0), 0.0, sign)
+    sign = jnp.where((slab_index() == 0) & (((lane >> 4) & 3) == 0), 0.0, sign)
     scale = factors[...]
     kept_cosine = scale * (cosine + sign * pltpu.roll(sine, 64, 1))
     kept_sine = scale * (sine - sign * pltpu.roll(cosine, 64, 1))
@@ -209,7 +214,6 @@
 
 def on_device(sizes, features, target, out_weight, rotation, blocks, wedge):
     slab = tuple(name for name, _ in PARTS["slab"])
-    place = lax.axis_index(slab).astype(jnp.int32).reshape(1)
     features = features.reshape(C * ROWS, N)
     target = target.reshape(ROWS, N)
     inputs = [
@@ -219,7 +223,7 @@
     lines, factors, features, fwd_high, fwd_low, along_high, along_low = call(
         forward_x,
         [((128, 128), F32), ((N, 128), F32), ((C * ROWS, N), BF16)] + [(table.shape, BF16) for table in inputs[5:]],
-        "ss" + "h" * 9 + ">" + "v" * 7,
+        "s" + "h" * 9 + ">" + "v" * 7,
         [
             pltpu.SMEM((C,), F32),
             pltpu.SMEM((2, NB), jnp.int32),
@@ -228,10 +232,10 @@
             pltpu.SemaphoreType.DMA((8 + CHUNKS,)),
         ],
         (200_000_000, 3_000_000),
-    )(place, rotation, *inputs)
+    )(rotation, *inputs)
     lines = lax.all_to_all(lines.reshape(SLABS, 4, 128), slab, 0, 0, tiled=True).reshape(128, 128)
-    (back,) = call(filter_z, [((128, 128), F32)], "svvvv>v", (), (200_000_000, 2_000_000))(
-        place, lines, factors, along_high, along_low
+    (back,) = call(filter_z, [((128, 128), F32)], "vvvv>v", (), (200_000_000, 2_000_000))(
+        lines, factors, along_high, along_low
     )
     back = lax.all_to_all(back.reshape(SLABS, 4, 128), slab, 0, 0, tiled=True).reshape(128, 128)
     far = math.prod(sizes[name] for name in FAR)

time: 84.1 us -> 84.1 us (level)
  no operation moved by 1% of the time
where the time goes in v3:
time: 84.1 us; the launch traced here: 83.9 us
  blocking collectives  77.1 us (92%)
  Pallas kernels  4.83 us (6%)
  between operations  1.3 us (2%)
    all_to_all x1, blocking collectives, on_device(): lax.all_to_all(lines.reshape(SLABS, 4, 128), slab, 0, 0, tiled=True)  29.4 us
    all_to_all x1, blocking collectives, on_device(): sums = lax.all_to_all(sums.reshape(far, 1, 128), FAR, 0, 0, tiled=True)  19.6 us
    all_to_all x1, blocking collectives, on_device(): lax.all_to_all(back.reshape(SLABS, 4, 128), slab, 0, 0, tiled=True)  15.5 us
    all_to_all x1, blocking collectives, on_device(): sums = lax.all_to_all(sums, NEAR, 0, 0, tiled=True)  12.7 us
    pallas_call x1, Pallas kernels, on_device(): call(forward_x, [((128, 128), F32), ((N, 128), F32), ((C * ROWS, N), BF16...  2.49 us

profile of v3, /device:TPU:1, one launch (start us, length us, event | category | flops | bytes accessed | tf_op | source)
XLA Modules:
  0.0 83.9 jit_solution(2129784023963660925)
XLA Ops:
  1.3 2.5 %shard_map.113 = (f32[128,128]{1,0:T(8,128)S(1)}, f32[256,128]{1,0:T(8,128)S(1)}, bf16[4096,256]{1,0:T(8,128)(2,1)S(1)}, bf16[256,256]{1,0:T(8,128)(2,1)S(1)}, b...) custom-call(s32[1]{0:T(128)S(6)} %copy.16.turn, f32[64]{0:T(128)} %weight_hbm.1, ...), custom_call_target="tpu_custom_call" | custom-call | flops 200000000 | bytes 3000000 | tf_op jit(solution)/shard_map/pallas_call | solution.py:223
  3.8 29.4 %all_to_all.20 = f32[32,4,128]{2,1,0:T(4,128)S(1)} all-to-all(f32[32,4,128]{2,1,0:T(4,128)S(1)} %bitcast.15), channel_id=1, replica_groups=mesh['y'=4,'xh'=2,'core'=2,'z'=16,'xl'=2] {'z','xl'}, dimensions={0} | all-to-all | bytes 131072 | tf_op jit(solution)/shard_map/all_to_all | solution.py:236
  33.2 1.3 %shard_map.114 = f32[128,128]{1,0:T(8,128)S(1)} custom-call(f32[128,128]{1,0:T(8,128)S(1)} %bitcast.13, f32[256,128]{1,0:T(8,128)S(1)} %get-tuple-element.12.factors, bf16[512,256]{1,0:T(8,128)(2,1)S(1)} %get-tuple-element.13.along_high, bf16[512,256]{1,0:T(8,128)(2,1)S(1)} %get-tuple-element.14.along_low), custom_call_target="tpu_custom_call" | custom-call | flops 200000000 | bytes 2000000 | tf_op jit(solution)/shard_map/pallas_call | solution.py:237
  34.4 15.5 %all_to_all.21 = f32[32,4,128]{2,1,0:T(4,128)S(1)} all-to-all(f32[32,4,128]{2,1,0:T(4,128)S(1)} %bitcast.14), channel_id=1, replica_groups=mesh['y'=4,'xh'=2,'core'=2,'z'=16,'xl'=2] {'z','xl'}, dimensions={0} | all-to-all | bytes 131072 | tf_op jit(solution)/shard_map/all_to_all | solution.py:240
  49.9 1.1 %shard_map.115 = (f32[64,256]{1,0:T(8,128)}, f32[64,128]{1,0:T(8,128)S(1)}) custom-call(f32[128,128]{1,0:T(8,128)S(1)} %bitcast.12, bf16[4096,256]{1,0:T(8,128)(2,1)S(1)} %get-tuple-element.15.features, bf16[256,256]{1,0:T(8,128)(2,1)S(1)} %get-tuple-element.16.fwd_high, bf16[256,256]{1,0:T(8,128)(2,1)S(1)} %get-tuple-element.17.fwd_low), custom_call_target="tpu_custom_call" | custom-call | flops 200000000 | bytes 3000000 | tf_op jit(solution)/shard_map/pallas_call | solution.py:243
  51.0 19.6 %all_to_all.22 = f32[64,1,128]{2,1,0:T(1,128)S(1)} all-to-all(f32[64,1,128]{2,1,0:T(1,128)S(1)} %bitcast.16), channel_id=1, replica_groups=mesh['y'=4,'xh'=2,'core'=2,'z'=16,'xl'=2] {'core','z','xl'}, dimensions={0} | all-to-all | bytes 65536 | tf_op jit(solution)/shard_map/all_to_all | solution.py:250
  70.6 0.1 reduce_sum.18
  70.7 12.7 %all_to_all.23 = f32[8,1,128]{2,1,0:T(1,128)S(1)} all-to-all(f32[8,1,128]{2,1,0:T(1,128)S(1)} %broadcast_in_dim.2), channel_id=1, replica_groups=mesh['y'=4,'xh'=2,'core'=2,'z'=16,'xl'=2] {'y','xh'}, dimensions={0} | all-to-all | bytes 8192 | tf_op jit(solution)/shard_map/all_to_all | solution.py:253
  83.4 0.5 slice_multiply_fusion
  (2 shorter events, 0.0 us)

commit v4 on v3

--- a/solution.py
+++ b/solution.py
@@ -19,9 +19,12 @@
 YP = 8
 ROWS = ZL * YP
 CHUNKS = 4
-PARTS = {"dp": (("y", 4), ("xh", 2), ("core", 2)), "slab": (("z", 16), ("xl", 2))}
+PARTS = {"dp": (("y", 4), ("xh", 2), ("core", 2)), "slab": (("zh", 4), ("zl", 4), ("xl", 2))}
+GROUPS = 4
+SETS = 4
 NEAR = ("y", "xh")
-FAR = ("core", "z", "xl")
+FAR = ("core", "zh", "zl", "xl")
+INSIDE = ("zl", "xl")
 
 F32, BF16 = jnp.float32, jnp.bfloat16
 VMEM_LIMIT = 16 * 1024 * 1024
@@ -41,8 +44,8 @@
     phase = (freq[:, None] * space[None, :]) % N * step
     real, imag = np.cos(phase), -np.sin(phase)
     imag[freq == 0] = np.cos(math.pi * space)
-    zp, m, i = np.meshgrid(np.arange(2), np.arange(4), np.arange(SLABS), indexing="ij")
-    depth = (8 * i + 2 * m + zp).reshape(-1)
+    zh, zp, m, k = np.meshgrid(np.arange(GROUPS), np.arange(2), np.arange(4), np.arange(8), indexing="ij")
+    depth = (64 * zh + 8 * k + 2 * m + zp).reshape(-1)
     phase = (depth[:, None] * depth[None, :]) % N * step
     along = np.concatenate([np.cos(phase), np.sin(phase)], 0)
     return halves(np.concatenate([real, imag], 0)) + halves(along)
@@ -70,11 +73,7 @@
     return result
 
 
-def slab_index():
-    return lax.axis_index(tuple(name for name, _ in PARTS["slab"])).astype(jnp.int32)
-
-
-def filter_weights(turn, place, blocks, wedge, out):
+def filter_weights(turn, blocks, wedge, out):
     kz = lax.broadcasted_iota(jnp.int32, (8, N), 0)
     kx = lane_of((8, N)) >> 6
     listed = jnp.zeros((8, N), jnp.bool_)
@@ -84,25 +83,20 @@
     mask = jnp.concatenate(
         [wedge[a * BLK : (a + 1) * BLK, :].astype(F32) * listed[a : a + 1, :] for a in range(N // BLK)], 0
     ).astype(BF16)
-    lane = lane_of((N, 128))
-    row = lax.broadcasted_iota(jnp.int32, (N, 128), 0)
-    quad = (lane >> 4) & 3
-    freq = 4 * place + quad
-    freq = jnp.where((freq == 0) & (lane >= 64), N // 2, freq)
+    lane = lane_of((N, N))
+    row = lax.broadcasted_iota(jnp.int32, (N, N), 0)
+    part, quad, odd_set, pair = (lane >> 6) & 1, (lane >> 4) & 3, (lane >> 3) & 1, lane >> 7
+    freq = 16 * lax.axis_index(INSIDE).astype(jnp.int32) + 8 * pair + 4 * odd_set + quad
+    freq = jnp.where((freq == 0) & (part == 1), N // 2, freq)
     plus = (row == freq).astype(F32).astype(BF16)
     minus = (row == ((N - freq) & (N - 1))).astype(F32).astype(BF16)
-    picks = jnp.concatenate([plus, minus], 1)
     odd = (turn & 1) == 1
-    plain = dot(mask, picks)
-    other = dot(mask, picks, ((0,), (0,)))
-    direct = jnp.where(odd, other[:, 128:], plain[:, :128])
-    mirror = jnp.where(odd, other[:, :128], plain[:, 128:]).astype(BF16)
-    r = lax.broadcasted_iota(jnp.int32, (N, N), 0)
-    p = 8 * (r & 31) + 2 * ((r >> 5) & 3) + (r >> 7)
-    k = lane_of((N, N))
-    keep = (k == p).astype(F32).astype(BF16)
-    flip = (((p + k) & (N - 1)) == 0).astype(F32).astype(BF16)
-    out[...] = dot(keep, direct.astype(BF16)) + dot(flip, mirror)
+    direct = jnp.where(odd, dot(mask, minus, ((0,), (0,))), dot(mask, plus)).astype(BF16)
+    mirror = jnp.where(odd, dot(mask, plus, ((0,), (0,))), dot(mask, minus)).astype(BF16)
+    p = (row & 192) + 8 * (row & 7) + 2 * ((row >> 3) & 3) + ((row >> 5) & 1)
+    keep = (lane == p).astype(F32).astype(BF16)
+    flip = (((p + lane) & (N - 1)) == 0).astype(F32).astype(BF16)
+    out[...] = dot(keep, direct) + dot(flip, mirror)
 
 
 def forward_x(
@@ -122,7 +116,7 @@
         copy.start()
     for copy in copies[:2]:
         copy.wait()
-    filter_weights(turn[0], slab_index(), blocks, wedge, factors)
+    filter_weights(turn[0], blocks, wedge, factors)
     for copy in copies[2 : len(small)]:
         copy.wait()
     total = -target[...].astype(F32)
@@ -141,31 +135,52 @@
     line = jnp.where(lane_of((128, 128)) < 64, line[:128], line[128:])
     pieces = [line[q * SLABS : (q + 1) * SLABS] for q in range(4)]
     for m in range(4):
-        lines[pl.ds(m, SLABS, stride=4), :] = regroup(pieces, m)
+        moved = regroup(pieces, m)
+        for zh in range(GROUPS):
+            lines[pl.ds(zh * 128 + m, SLABS, stride=4), :] = moved
 
 
 def filter_z(lines, factors, along_high, along_low, back):
-    even = jnp.concatenate([lines[pl.ds(m, SLABS, stride=4), :] for m in range(4)], 0)
-    data = jnp.concatenate([even, pltpu.roll(even, 120, 1)], 0)
-    high, low = split(data)
+    near = (lane_of((SLABS, 128)) & 8) == 0
+    halves_of = []
+    for pair in range(SETS // 2):
+        rows = {}
+        for m in range(4):
+            first = lines[pl.ds(8 * pair + m, SLABS, stride=16), :]
+            second = lines[pl.ds(8 * pair + 4 + m, SLABS, stride=16), :]
+            rows[0, m] = jnp.where(near, first, pltpu.roll(second, 8, 1))
+            rows[1, m] = jnp.where(near, pltpu.roll(first, 120, 1), second)
+        halves_of.append(
+            jnp.concatenate(
+                [rows[zp, m][8 * zh : 8 * zh + 8] for zh in range(GROUPS) for zp in range(2) for m in range(4)], 0
+            )
+        )
+    high, low = split(jnp.concatenate(halves_of, 1))
     freq = dot(along_high[...], high) + (dot(along_high[...], low) + dot(along_low[...], high))
-    cosine, sine = freq[:N], freq[N:]
     lane = lane_of((N, 128))
     sign = jnp.where(lane < 64, 1.0, -1.0)
-    sign = jnp.where((slab_index() == 0) & (((lane >> 4) & 3) == 0), 0.0, sign)
-    scale = factors[...]
-    kept_cosine = scale * (cosine + sign * pltpu.roll(sine, 64, 1))
-    kept_sine = scale * (sine - sign * pltpu.roll(cosine, 64, 1))
+    alone = (lax.axis_index(INSIDE) == 0) & ((lane & 56) == 0)
+    kept = []
+    for pair in range(SETS // 2):
+        cosine = freq[:N, 128 * pair : 128 * pair + 128]
+        sine = freq[N:, 128 * pair : 128 * pair + 128]
+        mix = jnp.where(alone, 0.0, sign) if pair == 0 else sign
+        scale = factors[:, 128 * pair : 128 * pair + 128]
+        kept.append((scale * (cosine + mix * pltpu.roll(sine, 64, 1)), scale * (sine - mix * pltpu.roll(cosine, 64, 1))))
+    own = lax.axis_index("zh") * 64
     depth = None
-    for kept, rows in ((kept_cosine, slice(0, N)), (kept_sine, slice(N, 2 * N))):
-        high, low = split(kept)
+    for part in range(2):
+        rows = pl.ds(pl.multiple_of(part * N + own, 64), 64)
+        high, low = split(jnp.concatenate([pieces[part] for pieces in kept], 1))
         term = dot(along_high[rows, :], high) + (dot(along_high[rows, :], low) + dot(along_low[rows, :], high))
         depth = term if depth is None else depth + term
-    lane = lane_of((SLABS, 128))
-    for m in range(4):
-        first = depth[m * SLABS : (m + 1) * SLABS]
-        second = depth[128 + m * SLABS : 128 + (m + 1) * SLABS]
-        back[pl.ds(m, SLABS, stride=4), :] = jnp.where((lane & 8) == 0, first, pltpu.roll(second, 8, 1))
+    near = (lane_of((8, 128)) & 8) == 0
+    for pair in range(SETS // 2):
+        for m in range(4):
+            even = depth[8 * m : 8 * m + 8, 128 * pair : 128 * pair + 128]
+            odd = depth[32 + 8 * m : 40 + 8 * m, 128 * pair : 128 * pair + 128]
+            back[pl.ds(8 * pair + m, 8, stride=16), :] = jnp.where(near, even, pltpu.roll(odd, 8, 1))
+            back[pl.ds(8 * pair + 4 + m, 8, stride=16), :] = jnp.where(near, pltpu.roll(even, 120, 1), odd)
 
 
 def inverse_x(lines, features, fwd_high, fwd_low, volume, sums, result, partial, sem):
@@ -222,7 +237,7 @@
     ]
     lines, factors, features, fwd_high, fwd_low, along_high, along_low = call(
         forward_x,
-        [((128, 128), F32), ((N, 128), F32), ((C * ROWS, N), BF16)] + [(table.shape, BF16) for table in inputs[5:]],
+        [((GROUPS * 128, 128), F32), ((N, N), F32), ((C * ROWS, N), BF16)] + [(table.shape, BF16) for table in inputs[5:]],
         "s" + "h" * 9 + ">" + "v" * 7,
         [
             pltpu.SMEM((C,), F32),
@@ -233,11 +248,11 @@
         ],
         (200_000_000, 3_000_000),
     )(rotation, *inputs)
-    lines = lax.all_to_all(lines.reshape(SLABS, 4, 128), slab, 0, 0, tiled=True).reshape(128, 128)
+    lines = lax.all_to_all(lines.reshape(SLABS, 16, 128), slab, 0, 0, tiled=True).reshape(SLABS * 16, 128)
     (back,) = call(filter_z, [((128, 128), F32)], "vvvv>v", (), (200_000_000, 2_000_000))(
         lines, factors, along_high, along_low
     )
-    back = lax.all_to_all(back.reshape(SLABS, 4, 128), slab, 0, 0, tiled=True).reshape(128, 128)
+    back = lax.all_to_all(back.reshape(8, 16, 128), INSIDE, 0, 0, tiled=True).reshape(128, 128)
     far = math.prod(sizes[name] for name in FAR)
     near = math.prod(sizes[name] for name in NEAR)
     volume, sums = call(

time: 84.1 us -> 86.2 us (1.025)
  blocking collectives: 77.1 us -> 79.4 us
    all_to_all x1, blocking collectives: 19.6 us -> 21.3 us  [on_device(): sums = lax.all_to_all(sums.reshape(far, 1, 128), FAR, 0, 0, tiled=True)]
where the time goes in v4:
time: 86.2 us; the launch traced here: 85.9 us
  blocking collectives  79.4 us (92%)
  Pallas kernels  4.66 us (5%)
  between operations  1.3 us (2%)
    all_to_all x1, blocking collectives, on_device(): lax.all_to_all(lines.reshape(SLABS, 16, 128), slab, 0, 0, tiled=True)  37.3 us
    all_to_all x1, blocking collectives, on_device(): sums = lax.all_to_all(sums.reshape(far, 1, 128), FAR, 0, 0, tiled=True)  21.3 us
    all_to_all x1, blocking collectives, on_device(): sums = lax.all_to_all(sums, NEAR, 0, 0, tiled=True)  12.7 us
    all_to_all x1, blocking collectives, on_device(): lax.all_to_all(back.reshape(8, 16, 128), INSIDE, 0, 0, tiled=True)  8.14 us
    pallas_call x1, Pallas kernels, on_device(): call(forward_x, [((GROUPS * 128, 128), F32), ((N, N), F32), ((C * ROWS, N...  2.59 us

profile of v4, /device:TPU:1, one launch (start us, length us, event | category | flops | bytes accessed | tf_op | source)
XLA Modules:
  0.0 85.9 jit_solution(2320116171342926162)
XLA Ops:
  1.3 2.6 %shard_map.113 = (f32[512,128]{1,0:T(8,128)S(1)}, f32[256,256]{1,0:T(8,128)S(1)}, bf16[4096,256]{1,0:T(8,128)(2,1)S(1)}, bf16[256,256]{1,0:T(8,128)(2,1)S(1)}, b...) custom-call(s32[1]{0:T(128)S(6)} %copy.16.turn, f32[64]{0:T(128)} %weight_hbm.1, ...), custom_call_target="tpu_custom_call" | custom-call | flops 200000000 | bytes 3000000 | tf_op jit(solution)/shard_map/pallas_call | solution.py:238
  3.9 37.3 %all_to_all.20 = f32[32,16,128]{2,1,0:T(8,128)S(1)} all-to-all(f32[32,16,128]{2,1,0:T(8,128)S(1)} %bitcast.15), channel_id=1, replica_groups=mesh['y'=4,'xh'=2,'core'=2,'zh'=4,'zl'=4,'xl'=2] {'zh','zl','xl'}, dimensions={0} | all-to-all | bytes 524288 | tf_op jit(solution)/shard_map/all_to_all | solution.py:251
  41.2 1.0 %shard_map.114 = f32[128,128]{1,0:T(8,128)S(1)} custom-call(f32[512,128]{1,0:T(8,128)S(1)} %bitcast.12, f32[256,256]{1,0:T(8,128)S(1)} %get-tuple-element.12.factors, bf16[512,256]{1,0:T(8,128)(2,1)S(1)} %get-tuple-element.13.along_high, bf16[512,256]{1,0:T(8,128)(2,1)S(1)} %get-tuple-element.14.along_low), custom_call_target="tpu_custom_call" | custom-call | flops 200000000 | bytes 2000000 | tf_op jit(solution)/shard_map/pallas_call | solution.py:252
  42.2 8.1 %all_to_all.21 = f32[8,16,128]{2,1,0:T(8,128)S(1)} all-to-all(f32[8,16,128]{2,1,0:T(8,128)S(1)} %bitcast.14), channel_id=1, replica_groups=mesh['y'=4,'xh'=2,'core'=2,'zh'=4,'zl'=4,'xl'=2] {'zl','xl'}, dimensions={0} | all-to-all | bytes 131072 | tf_op jit(solution)/shard_map/all_to_all | solution.py:255
  50.3 1.1 %shard_map.115 = (f32[64,256]{1,0:T(8,128)}, f32[64,128]{1,0:T(8,128)S(1)}) custom-call(f32[128,128]{1,0:T(8,128)S(1)} %bitcast.13, bf16[4096,256]{1,0:T(8,128)(2,1)S(1)} %get-tuple-element.15.features, bf16[256,256]{1,0:T(8,128)(2,1)S(1)} %get-tuple-element.16.fwd_high, bf16[256,256]{1,0:T(8,128)(2,1)S(1)} %get-tuple-element.17.fwd_low), custom_call_target="tpu_custom_call" | custom-call | flops 200000000 | bytes 3000000 | tf_op jit(solution)/shard_map/pallas_call | solution.py:258
  51.4 21.3 %all_to_all.22 = f32[64,1,128]{2,1,0:T(1,128)S(1)} all-to-all(f32[64,1,128]{2,1,0:T(1,128)S(1)} %bitcast.16), channel_id=1, replica_groups=mesh['y'=4,'xh'=2,'core'=2,'zh'=4,'zl'=4,'xl'=2] {'core','zh','zl','xl'}, dimensions={0} | all-to-all | bytes 65536 | tf_op jit(solution)/shard_map/all_to_all | solution.py:265
  72.7 0.1 reduce_sum.18
  72.8 12.7 %all_to_all.23 = f32[8,1,128]{2,1,0:T(1,128)S(1)} all-to-all(f32[8,1,128]{2,1,0:T(1,128)S(1)} %broadcast_in_dim.2), channel_id=1, replica_groups=mesh['y'=4,'xh'=2,'core'=2,'zh'=4,'zl'=4,'xl'=2] {'y','xh'}, dimensions={0} | all-to-all | bytes 8192 | tf_op jit(solution)/shard_map/all_to_all | solution.py:268
  85.4 0.5 slice_multiply_fusion
  (2 shorter events, 0.0 us)

commit v5 on v3

--- a/solution.py
+++ b/solution.py
@@ -18,7 +18,7 @@
 ZL = 8
 YP = 8
 ROWS = ZL * YP
-CHUNKS = 4
+CHUNKS = 8
 PARTS = {"dp": (("y", 4), ("xh", 2), ("core", 2)), "slab": (("z", 16), ("xl", 2))}
 NEAR = ("y", "xh")
 FAR = ("core", "z", "xl")
@@ -105,50 +105,57 @@
     out[...] = dot(keep, direct.astype(BF16)) + dot(flip, mirror)
 
 
-def forward_x(
-    turn, weight_hbm, blocks_hbm, wedge_hbm, features_hbm, target_hbm, *refs
-):
-    tables_hbm, (lines, factors, features), held = refs[:4], refs[4:7], refs[7:11]
-    weight, blocks, wedge, target, sems = refs[11:]
-    part = C * ROWS // CHUNKS
-    small = [(blocks_hbm, blocks), (wedge_hbm, wedge), (weight_hbm, weight), (target_hbm, target)]
-    pairs = list(small)
-    for k in range(CHUNKS):
-        rows = pl.ds(k * part, part)
-        pairs.append((features_hbm.at[rows], features.at[rows]))
-    pairs += list(zip(tables_hbm, held))
+def prepare(turn, blocks_hbm, wedge_hbm, high_hbm, low_hbm, factors, high, low, blocks, wedge, sems):
+    pairs = [(blocks_hbm, blocks), (wedge_hbm, wedge), (high_hbm, high), (low_hbm, low)]
     copies = [pltpu.make_async_copy(source, goal, sems.at[n]) for n, (source, goal) in enumerate(pairs)]
     for copy in copies:
         copy.start()
     for copy in copies[:2]:
         copy.wait()
     filter_weights(turn[0], slab_index(), blocks, wedge, factors)
-    for copy in copies[2 : len(small)]:
+    for copy in copies[2:]:
+        copy.wait()
+
+
+def forward_x(weight_hbm, target_hbm, features_hbm, high_hbm, low_hbm, lines, features, fwd_high, fwd_low, weight, target, sems):
+    part = C * ROWS // CHUNKS
+    pairs = [(weight_hbm, weight), (target_hbm, target)]
+    for k in range(CHUNKS):
+        rows = pl.ds(k * part, part)
+        pairs.append((features_hbm.at[rows], features.at[rows]))
+    pairs += [(high_hbm, fwd_high), (low_hbm, fwd_low)]
+    copies = [pltpu.make_async_copy(source, goal, sems.at[n]) for n, (source, goal) in enumerate(pairs)]
+    for copy in copies:
+        copy.start()
+    for copy in copies[:2]:
         copy.wait()
     total = -target[...].astype(F32)
     for k in range(CHUNKS):
-        copies[len(small) + k].wait()
+        copies[2 + k].wait()
         for c in range(k * C // CHUNKS, (k + 1) * C // CHUNKS):
             total = total + weight[c] * features[c * ROWS : (c + 1) * ROWS, :].astype(F32)
     high, low = split(total)
-    high = jnp.concatenate([high, high], 0)
-    low = jnp.concatenate([low, low], 0)
     nt = ((1,), (1,))
-    for copy in copies[len(small) + CHUNKS :]:
-        copy.wait()
-    fwd_high, fwd_low = held[:2]
-    line = dot(fwd_high[...], high, nt) + (dot(fwd_high[...], low, nt) + dot(fwd_low[...], high, nt))
+    for copy in copies[2 + CHUNKS :]:
+        copy.wait()
+    both = dot(fwd_high[...], jnp.concatenate([high, low], 0), nt)
+    line = dot(fwd_low[...], jnp.concatenate([high, high], 0), nt) + (both + pltpu.roll(both, 64, 1))
     line = jnp.where(lane_of((128, 128)) < 64, line[:128], line[128:])
     pieces = [line[q * SLABS : (q + 1) * SLABS] for q in range(4)]
     for m in range(4):
         lines[pl.ds(m, SLABS, stride=4), :] = regroup(pieces, m)
 
 
+def three(left_high, left_low, right):
+    high, low = split(right)
+    both = dot(left_high, jnp.concatenate([high, low], 1))
+    return dot(left_low, high) + (both[:, :128] + both[:, 128:])
+
+
 def filter_z(lines, factors, along_high, along_low, back):
     even = jnp.concatenate([lines[pl.ds(m, SLABS, stride=4), :] for m in range(4)], 0)
     data = jnp.concatenate([even, pltpu.roll(even, 120, 1)], 0)
-    high, low = split(data)
-    freq = dot(along_high[...], high) + (dot(along_high[...], low) + dot(along_low[...], high))
+    freq = three(along_high[...], along_low[...], data)
     cosine, sine = freq[:N], freq[N:]
     lane = lane_of((N, 128))
     sign = jnp.where(lane < 64, 1.0, -1.0)
@@ -156,11 +163,7 @@
     scale = factors[...]
     kept_cosine = scale * (cosine + sign * pltpu.roll(sine, 64, 1))
     kept_sine = scale * (sine - sign * pltpu.roll(cosine, 64, 1))
-    depth = None
-    for kept, rows in ((kept_cosine, slice(0, N)), (kept_sine, slice(N, 2 * N))):
-        high, low = split(kept)
-        term = dot(along_high[rows, :], high) + (dot(along_high[rows, :], low) + dot(along_low[rows, :], high))
-        depth = term if depth is None else depth + term
+    depth = three(along_high[:N, :], along_low[:N, :], kept_cosine) + three(along_high[N:, :], along_low[N:, :], kept_sine)
     lane = lane_of((SLABS, 128))
     for m in range(4):
         first = depth[m * SLABS : (m + 1) * SLABS]
@@ -174,7 +177,8 @@
     line = jnp.concatenate([line[:64], line[64:]], 1)
     line = line * jnp.where((lane_of((ROWS, N)) & 127) == 0, 1.0 / (N * N), 2.0 / (N * N))
     high, low = split(line)
-    values = dot(high, fwd_high[...]) + (dot(low, fwd_high[...]) + dot(high, fwd_low[...]))
+    both = dot(jnp.concatenate([high, low], 0), fwd_high[...])
+    values = both[:ROWS] + (both[ROWS:] + dot(high, fwd_low[...]))
     result[...] = values
     leave = pltpu.make_async_copy(result, volume, sem)
     leave.start()
@@ -212,27 +216,30 @@
     )
 
 
+def hbm(array):
+    return pltpu.with_memory_space_constraint(array, pltpu.HBM)
+
+
 def on_device(sizes, features, target, out_weight, rotation, blocks, wedge):
     slab = tuple(name for name, _ in PARTS["slab"])
     features = features.reshape(C * ROWS, N)
     target = target.reshape(ROWS, N)
-    inputs = [
-        pltpu.with_memory_space_constraint(jnp.asarray(each), pltpu.HBM)
-        for each in (out_weight, blocks.T, wedge, features, target) + tables()
-    ]
-    lines, factors, features, fwd_high, fwd_low, along_high, along_low = call(
+    fwd_high, fwd_low, along_high, along_low = [hbm(jnp.asarray(table)) for table in tables()]
+    lines, features, fwd_high, fwd_low = call(
         forward_x,
-        [((128, 128), F32), ((N, 128), F32), ((C * ROWS, N), BF16)] + [(table.shape, BF16) for table in inputs[5:]],
-        "s" + "h" * 9 + ">" + "v" * 7,
-        [
-            pltpu.SMEM((C,), F32),
-            pltpu.SMEM((2, NB), jnp.int32),
-            pltpu.VMEM((N, N), jnp.int32),
-            pltpu.VMEM((ROWS, N), BF16),
-            pltpu.SemaphoreType.DMA((8 + CHUNKS,)),
-        ],
+        [((128, 128), F32), ((C * ROWS, N), BF16), (fwd_high.shape, BF16), (fwd_low.shape, BF16)],
+        "hhhhh>vvvv",
+        [pltpu.SMEM((C,), F32), pltpu.VMEM((ROWS, N), BF16), pltpu.SemaphoreType.DMA((4 + CHUNKS,))],
         (200_000_000, 3_000_000),
-    )(rotation, *inputs)
+    )(hbm(out_weight), hbm(target), hbm(features), fwd_high, fwd_low)
+    rotation, lines = lax.optimization_barrier((rotation, lines))
+    factors, along_high, along_low = call(
+        prepare,
+        [((N, 128), F32), (along_high.shape, BF16), (along_low.shape, BF16)],
+        "shhhh>vvv",
+        [pltpu.SMEM((2, NB), jnp.int32), pltpu.VMEM((N, N), jnp.int32), pltpu.SemaphoreType.DMA((4,))],
+        (200_000_000, 3_000_000),
+    )(rotation, hbm(blocks.T), hbm(wedge), along_high, along_low)
     lines = lax.all_to_all(lines.reshape(SLABS, 4, 128), slab, 0, 0, tiled=True).reshape(128, 128)
     (back,) = call(filter_z, [((128, 128), F32)], "vvvv>v", (), (200_000_000, 2_000_000))(
         lines, factors, along_high, along_low

time: 84.1 us -> 83.5 us (level)
  blocking collectives: 77.1 us -> 47.7 us
  starting transfers between devices: 0 us -> 17 us
  waiting for transfers between devices: 0 us -> 10.5 us
  Pallas kernels: 4.83 us -> 5.99 us
    all_to_all x1 -> x0, blocking collectives: 29.4 us -> none  [on_device(): lax.all_to_all(lines.reshape(SLABS, 4, 128), slab, 0, 0, tiled=True)]
    all_to_all x0 -> x1, starting transfers between devices: none -> 17 us  [on_device(): lax.all_to_all(lines.reshape(SLABS, 4, 128), slab, 0, 0, tiled=True)]
    all_to_all x0 -> x1, waiting for transfers between devices: none -> 10.5 us  [on_device(): lax.all_to_all(lines.reshape(SLABS, 4, 128), slab, 0, 0, tiled=True)]
    pallas_call x1 -> x2, Pallas kernels: 2.49 us -> 4.19 us  [the longest x1 2.71 us: on_device(): call(forward_x, [((128, 128), F32), ((C * ROWS, N), BF16), (fwd_high.shap...]
  transfers between devices with their start and end apart: 0 -> 1, of which waited for: 0 -> 1; matrix products, arithmetic and copies ran while one was open for 0% -> 0% of each run, Pallas kernels for 0% -> 2%
where the time goes in v5:
time: 83.5 us; the launch traced here: 83.1 us
  blocking collectives  47.7 us (57%)
  starting transfers between devices  17 us (20%)
  waiting for transfers between devices  10.5 us (13%)
  Pallas kernels  5.99 us (7%)
  between operations  1.32 us (2%)
    all_to_all x1, blocking collectives, on_device(): sums = lax.all_to_all(sums.reshape(far, 1, 128), FAR, 0, 0, tiled=True)  19.6 us
    all_to_all x1, starting transfers between devices, on_device(): lax.all_to_all(lines.reshape(SLABS, 4, 128), slab, 0, 0, tiled=True)  17 us
    all_to_all x1, blocking collectives, on_device(): lax.all_to_all(back.reshape(SLABS, 4, 128), slab, 0, 0, tiled=True)  15.5 us
    all_to_all x1, blocking collectives, on_device(): sums = lax.all_to_all(sums, NEAR, 0, 0, tiled=True)  12.7 us
    all_to_all x1, waiting for transfers between devices, on_device(): lax.all_to_all(lines.reshape(SLABS, 4, 128), slab, 0, 0, tiled=True)  10.5 us
    pallas_call x1, Pallas kernels, on_device(): call(forward_x, [((128, 128), F32), ((C * ROWS, N), BF16), (fwd_high.shap...  2.71 us
  transfers between devices with their start and end apart: 1, of which 1 were waited for; matrix products, arithmetic and copies ran while one was open for 0% of the time, Pallas kernels for 2%

profile of v5, /device:TPU:1, one launch (start us, length us, event | category | flops | bytes accessed | tf_op | source)
XLA Modules:
  0.0 83.1 jit_solution(16918976106563075844)
XLA Ops:
  0.6 2.7 %shard_map.113 = (f32[128,128]{1,0:T(8,128)}, bf16[4096,256]{1,0:T(8,128)(2,1)S(1)}, bf16[256,256]{1,0:T(8,128)(2,1)S(1)}, bf16[256,256]{1,0:T(8,128)(2,1)S(1)}) custom-call(f32[64]{0:T(128)} %weight_hbm.1, bf16[64,256]{1,0:T(8,128)(2,1)} %bitcast.17, bf16[4096,256]{1,0:T(8,128)(2,1)} %bitcast.16, bf16[256,256]{1,0:T(8,128)(2,1)} %constant.12.clone.high_hbm, ...), custom_call_target="tpu_custom_call" | custom-call | flops 200000000 | bytes 3000000 | tf_op jit(solution)/shard_map/pallas_call | solution.py:228
  3.4 17.0 %all-to-all-start = ((f32[32,4,128]{2,1,0:T(4,128)}), f32[32,4,128]{2,1,0:T(4,128)S(1)}, u32[]{:S(2)}, u32[]{:S(2)}) async-start(f32[32,4,128]{2,1,0:T(4,128)} %bitcast.2), calls=%async_computation | async-start | bytes 131072 | tf_op jit(solution)/shard_map/all_to_all | solution.py:243
  21.0 1.5 %shard_map.114 = (f32[256,128]{1,0:T(8,128)S(1)}, bf16[512,256]{1,0:T(8,128)(2,1)S(1)}, bf16[512,256]{1,0:T(8,128)(2,1)S(1)}) custom-call(s32[1]{0:T(128)S(6)} %copy.16.turn, s32[2,8]{1,0:T(2,128)} %bitcast.19, s32[256,256]{1,0:T(8,128)} %wedge_hbm.1, bf16[512,256]{1,0:T(8,128)(2,1)} %constant.14.clone.high_hbm, bf16[512,256]{1,0:T(8,128)(2,1)} %constant.15.clone.low_hbm), custom_call_target="tpu_custom_call" | custom-call | flops 200000000 | bytes 3000000 | tf_op jit(solution)/shard_map/pallas_call | solution.py:236
  22.5 10.5 %all-to-all-done = f32[32,4,128]{2,1,0:T(4,128)S(1)} async-done(((f32[32,4,128]{2,1,0:T(4,128)}), f32[32,4,128]{2,1,0:T(4,128)S(1)}, u32[]{:S(2)}, u32[]{:S(2)}) %all-to-all-start) | async-done | bytes 65568 | tf_op jit(solution)/shard_map/all_to_all | solution.py:243
  33.0 0.8 shard_map.115
  33.7 15.5 %all_to_all.20 = f32[32,4,128]{2,1,0:T(4,128)S(1)} all-to-all(f32[32,4,128]{2,1,0:T(4,128)S(1)} %bitcast.14), channel_id=1, replica_groups=mesh['y'=4,'xh'=2,'core'=2,'z'=16,'xl'=2] {'z','xl'}, dimensions={0} | all-to-all | bytes 131072 | tf_op jit(solution)/shard_map/all_to_all | solution.py:247
  49.2 1.0 %shard_map.116 = (f32[64,256]{1,0:T(8,128)}, f32[64,128]{1,0:T(8,128)S(1)}) custom-call(f32[128,128]{1,0:T(8,128)S(1)} %bitcast.13, bf16[4096,256]{1,0:T(8,128)(2,1)S(1)} %get-tuple-element.19.features, bf16[256,256]{1,0:T(8,128)(2,1)S(1)} %get-tuple-element.20.fwd_high, bf16[256,256]{1,0:T(8,128)(2,1)S(1)} %get-tuple-element.21.fwd_low), custom_call_target="tpu_custom_call" | custom-call | flops 200000000 | bytes 3000000 | tf_op jit(solution)/shard_map/pallas_call | solution.py:250
  50.2 19.6 %all_to_all.21 = f32[64,1,128]{2,1,0:T(1,128)S(1)} all-to-all(f32[64,1,128]{2,1,0:T(1,128)S(1)} %bitcast.15), channel_id=1, replica_groups=mesh['y'=4,'xh'=2,'core'=2,'z'=16,'xl'=2] {'core','z','xl'}, dimensions={0} | all-to-all | bytes 65536 | tf_op jit(solution)/shard_map/all_to_all | solution.py:257
  69.9 0.1 reduce_sum.18
  69.9 12.7 %all_to_all.22 = f32[8,1,128]{2,1,0:T(1,128)S(1)} all-to-all(f32[8,1,128]{2,1,0:T(1,128)S(1)} %broadcast_in_dim.2), channel_id=1, replica_groups=mesh['y'=4,'xh'=2,'core'=2,'z'=16,'xl'=2] {'y','xh'}, dimensions={0} | all-to-all | bytes 8192 | tf_op jit(solution)/shard_map/all_to_all | solution.py:260
  82.6 0.5 slice_multiply_fusion
  (2 shorter events, 0.0 us)
Async XLA Ops:
  3.4 29.6 %all-to-all-start = ((f32[32,4,128]{2,1,0:T(4,128)}), f32[32,4,128]{2,1,0:T(4,128)S(1)}, u32[]{:S(2)}, u32[]{:S(2)}) async-start(f32[32,4,128]{2,1,0:T(4,128)} %bitcast.2), calls=%async_computation | async-start | bytes 131072 | tf_op jit(solution)/shard_map/all_to_all | solution.py:243

commit v6 on v5

--- a/solution.py
+++ b/solution.py
@@ -19,9 +19,12 @@
 YP = 8
 ROWS = ZL * YP
 CHUNKS = 8
-PARTS = {"dp": (("y", 4), ("xh", 2), ("core", 2)), "slab": (("z", 16), ("xl", 2))}
+PARTS = {"dp": (("y", 4), ("xh", 2), ("core", 2)), "slab": (("zh", 4), ("zl", 4), ("xl", 2))}
+GROUPS = 4
+SETS = 4
 NEAR = ("y", "xh")
-FAR = ("core", "z", "xl")
+FAR = ("core", "zh", "zl", "xl")
+INSIDE = ("zl", "xl")
 
 F32, BF16 = jnp.float32, jnp.bfloat16
 VMEM_LIMIT = 16 * 1024 * 1024
@@ -41,8 +44,8 @@
     phase = (freq[:, None] * space[None, :]) % N * step
     real, imag = np.cos(phase), -np.sin(phase)
     imag[freq == 0] = np.cos(math.pi * space)
-    zp, m, i = np.meshgrid(np.arange(2), np.arange(4), np.arange(SLABS), indexing="ij")
-    depth = (8 * i + 2 * m + zp).reshape(-1)
+    zh, zp, m, k = np.meshgrid(np.arange(GROUPS), np.arange(2), np.arange(4), np.arange(8), indexing="ij")
+    depth = (64 * zh + 8 * k + 2 * m + zp).reshape(-1)
     phase = (depth[:, None] * depth[None, :]) % N * step
     along = np.concatenate([np.cos(phase), np.sin(phase)], 0)
     return halves(np.concatenate([real, imag], 0)) + halves(along)
@@ -70,11 +73,7 @@
     return result
 
 
-def slab_index():
-    return lax.axis_index(tuple(name for name, _ in PARTS["slab"])).astype(jnp.int32)
-
-
-def filter_weights(turn, place, blocks, wedge, out):
+def filter_weights(turn, blocks, wedge, out):
     kz = lax.broadcasted_iota(jnp.int32, (8, N), 0)
     kx = lane_of((8, N)) >> 6
     listed = jnp.zeros((8, N), jnp.bool_)
@@ -84,25 +83,20 @@
     mask = jnp.concatenate(
         [wedge[a * BLK : (a + 1) * BLK, :].astype(F32) * listed[a : a + 1, :] for a in range(N // BLK)], 0
     ).astype(BF16)
-    lane = lane_of((N, 128))
-    row = lax.broadcasted_iota(jnp.int32, (N, 128), 0)
-    quad = (lane >> 4) & 3
-    freq = 4 * place + quad
-    freq = jnp.where((freq == 0) & (lane >= 64), N // 2, freq)
+    lane = lane_of((N, N))
+    row = lax.broadcasted_iota(jnp.int32, (N, N), 0)
+    part, quad, odd_set, pair = (lane >> 6) & 1, (lane >> 4) & 3, (lane >> 3) & 1, lane >> 7
+    freq = 16 * lax.axis_index(INSIDE).astype(jnp.int32) + 8 * pair + 4 * odd_set + quad
+    freq = jnp.where((freq == 0) & (part == 1), N // 2, freq)
     plus = (row == freq).astype(F32).astype(BF16)
     minus = (row == ((N - freq) & (N - 1))).astype(F32).astype(BF16)
-    picks = jnp.concatenate([plus, minus], 1)
     odd = (turn & 1) == 1
-    plain = dot(mask, picks)
-    other = dot(mask, picks, ((0,), (0,)))
-    direct = jnp.where(odd, other[:, 128:], plain[:, :128])
-    mirror = jnp.where(odd, other[:, :128], plain[:, 128:]).astype(BF16)
-    r = lax.broadcasted_iota(jnp.int32, (N, N), 0)
-    p = 8 * (r & 31) + 2 * ((r >> 5) & 3) + (r >> 7)
-    k = lane_of((N, N))
-    keep = (k == p).astype(F32).astype(BF16)
-    flip = (((p + k) & (N - 1)) == 0).astype(F32).astype(BF16)
-    out[...] = dot(keep, direct.astype(BF16)) + dot(flip, mirror)
+    direct = jnp.where(odd, dot(mask, minus, ((0,), (0,))), dot(mask, plus)).astype(BF16)
+    mirror = jnp.where(odd, dot(mask, plus, ((0,), (0,))), dot(mask, minus)).astype(BF16)
+    p = (row & 192) + 8 * (row & 7) + 2 * ((row >> 3) & 3) + ((row >> 5) & 1)
+    keep = (lane == p).astype(F32).astype(BF16)
+    flip = (((p + lane) & (N - 1)) == 0).astype(F32).astype(BF16)
+    out[...] = dot(keep, direct) + dot(flip, mirror)
 
 
 def prepare(turn, blocks_hbm, wedge_hbm, high_hbm, low_hbm, factors, high, low, blocks, wedge, sems):
@@ -112,7 +106,7 @@
         copy.start()
     for copy in copies[:2]:
         copy.wait()
-    filter_weights(turn[0], slab_index(), blocks, wedge, factors)
+    filter_weights(turn[0], blocks, wedge, factors)
     for copy in copies[2:]:
         copy.wait()
 
@@ -148,31 +142,49 @@
 
 def three(left_high, left_low, right):
     high, low = split(right)
-    both = dot(left_high, jnp.concatenate([high, low], 1))
-    return dot(left_low, high) + (both[:, :128] + both[:, 128:])
+    return dot(left_high, high) + (dot(left_high, low) + dot(left_low, high))
 
 
 def filter_z(lines, factors, along_high, along_low, back):
-    even = jnp.concatenate([lines[pl.ds(m, SLABS, stride=4), :] for m in range(4)], 0)
-    data = jnp.concatenate([even, pltpu.roll(even, 120, 1)], 0)
+    near = (lane_of((8, 128)) & 8) == 0
+    own = []
+    for pair in range(SETS // 2):
+        rows = {}
+        for m in range(4):
+            first = lines[pl.ds(8 * pair + m, 8, stride=16), :]
+            second = lines[pl.ds(8 * pair + 4 + m, 8, stride=16), :]
+            rows[0, m] = jnp.where(near, first, pltpu.roll(second, 8, 1))
+            rows[1, m] = jnp.where(near, pltpu.roll(first, 120, 1), second)
+        own.append(jnp.concatenate([rows[zp, m] for zp in range(2) for m in range(4)], 0))
+    own = jnp.concatenate(own, 1)
+    group = lax.axis_index("zh")
+    data = jnp.concatenate([jnp.where(group == zh, own, 0.0) for zh in range(GROUPS)], 0)
     freq = three(along_high[...], along_low[...], data)
-    cosine, sine = freq[:N], freq[N:]
     lane = lane_of((N, 128))
     sign = jnp.where(lane < 64, 1.0, -1.0)
-    sign = jnp.where((slab_index() == 0) & (((lane >> 4) & 3) == 0), 0.0, sign)
-    scale = factors[...]
-    kept_cosine = scale * (cosine + sign * pltpu.roll(sine, 64, 1))
-    kept_sine = scale * (sine - sign * pltpu.roll(cosine, 64, 1))
+    alone = (lax.axis_index(INSIDE) == 0) & ((lane & 56) == 0)
+    kept = []
+    for pair in range(SETS // 2):
+        cosine = freq[:N, 128 * pair : 128 * pair + 128]
+        sine = freq[N:, 128 * pair : 128 * pair + 128]
+        mix = jnp.where(alone, 0.0, sign) if pair == 0 else sign
+        scale = factors[:, 128 * pair : 128 * pair + 128]
+        kept.append((scale * (cosine + mix * pltpu.roll(sine, 64, 1)), scale * (sine - mix * pltpu.roll(cosine, 64, 1))))
+    kept_cosine, kept_sine = (jnp.concatenate([pieces[part] for pieces in kept], 1) for part in range(2))
     depth = three(along_high[:N, :], along_low[:N, :], kept_cosine) + three(along_high[N:, :], along_low[N:, :], kept_sine)
-    lane = lane_of((SLABS, 128))
-    for m in range(4):
-        first = depth[m * SLABS : (m + 1) * SLABS]
-        second = depth[128 + m * SLABS : 128 + (m + 1) * SLABS]
-        back[pl.ds(m, SLABS, stride=4), :] = jnp.where((lane & 8) == 0, first, pltpu.roll(second, 8, 1))
+    for zh in range(GROUPS):
+        for pair in range(SETS // 2):
+            for m in range(4):
+                row = 64 * zh + 8 * m
+                even = depth[row : row + 8, 128 * pair : 128 * pair + 128]
+                odd = depth[row + 32 : row + 40, 128 * pair : 128 * pair + 128]
+                goal = 128 * zh + 8 * pair + m
+                back[pl.ds(goal, 8, stride=16), :] = jnp.where(near, even, pltpu.roll(odd, 8, 1))
+                back[pl.ds(goal + 4, 8, stride=16), :] = jnp.where(near, pltpu.roll(even, 120, 1), odd)
 
 
 def inverse_x(lines, features, fwd_high, fwd_low, volume, sums, result, partial, sem):
-    blocks = [lines[pl.ds(m, SLABS, stride=4), :] for m in range(4)]
+    blocks = [sum(lines[pl.ds(128 * zh + m, SLABS, stride=4), :] for zh in range(GROUPS)) for m in range(4)]
     line = jnp.concatenate([regroup(blocks, q) for q in range(4)], 0).T
     line = jnp.concatenate([line[:64], line[64:]], 1)
     line = line * jnp.where((lane_of((ROWS, N)) & 127) == 0, 1.0 / (N * N), 2.0 / (N * N))
@@ -235,16 +247,16 @@
     rotation, lines = lax.optimization_barrier((rotation, lines))
     factors, along_high, along_low = call(
         prepare,
-        [((N, 128), F32), (along_high.shape, BF16), (along_low.shape, BF16)],
+        [((N, N), F32), (along_high.shape, BF16), (along_low.shape, BF16)],
         "shhhh>vvv",
         [pltpu.SMEM((2, NB), jnp.int32), pltpu.VMEM((N, N), jnp.int32), pltpu.SemaphoreType.DMA((4,))],
         (200_000_000, 3_000_000),
     )(rotation, hbm(blocks.T), hbm(wedge), along_high, along_low)
-    lines = lax.all_to_all(lines.reshape(SLABS, 4, 128), slab, 0, 0, tiled=True).reshape(128, 128)
-    (back,) = call(filter_z, [((128, 128), F32)], "vvvv>v", (), (200_000_000, 2_000_000))(
+    lines = lax.all_to_all(lines.reshape(8, 16, 128), INSIDE, 0, 0, tiled=True).reshape(128, 128)
+    (back,) = call(filter_z, [((GROUPS * 128, 128), F32)], "vvvv>v", (), (200_000_000, 2_000_000))(
         lines, factors, along_high, along_low
     )
-    back = lax.all_to_all(back.reshape(SLABS, 4, 128), slab, 0, 0, tiled=True).reshape(128, 128)
+    back = lax.all_to_all(back.reshape(SLABS, 16, 128), slab, 0, 0, tiled=True).reshape(GROUPS * 128, 128)
     far = math.prod(sizes[name] for name in FAR)
     near = math.prod(sizes[name] for name in NEAR)
     volume, sums = call(

time: 83.5 us -> 84 us (level)
  blocking collectives: 47.7 us -> 64.2 us
  starting transfers between devices: 17 us -> 7.39 us
  waiting for transfers between devices: 10.5 us -> 3.39 us
    all_to_all x1, blocking collectives: 15.5 us -> 31 us  [on_device(): lax.all_to_all(back.reshape(SLABS, 16, 128), slab, 0, 0, tiled=True)]
    all_to_all x1, starting transfers between devices: 17 us -> 7.39 us  [on_device(): lax.all_to_all(lines.reshape(8, 16, 128), INSIDE, 0, 0, tiled=True)]
    all_to_all x1, waiting for transfers between devices: 10.5 us -> 3.39 us  [on_device(): lax.all_to_all(lines.reshape(8, 16, 128), INSIDE, 0, 0, tiled=True)]
    all_to_all x1, blocking collectives: 19.6 us -> 20.6 us  [on_device(): sums = lax.all_to_all(sums.reshape(far, 1, 128), FAR, 0, 0, tiled=True)]
where the time goes in v6:
time: 84 us; the launch traced here: 83.7 us
  blocking collectives  64.2 us (76%)
  starting transfers between devices  7.39 us (9%)
  Pallas kernels  6.76 us (8%)
  waiting for transfers between devices  3.39 us (4%)
  between operations  1.32 us (2%)
    all_to_all x1, blocking collectives, on_device(): lax.all_to_all(back.reshape(SLABS, 16, 128), slab, 0, 0, tiled=True)  31 us
    all_to_all x1, blocking collectives, on_device(): sums = lax.all_to_all(sums.reshape(far, 1, 128), FAR, 0, 0, tiled=True)  20.6 us
    all_to_all x1, blocking collectives, on_device(): sums = lax.all_to_all(sums, NEAR, 0, 0, tiled=True)  12.7 us
    all_to_all x1, starting transfers between devices, on_device(): lax.all_to_all(lines.reshape(8, 16, 128), INSIDE, 0, 0, tiled=True)  7.39 us
    all_to_all x1, waiting for transfers between devices, on_device(): lax.all_to_all(lines.reshape(8, 16, 128), INSIDE, 0, 0, tiled=True)  3.39 us
    pallas_call x1, Pallas kernels, on_device(): call(forward_x, [((128, 128), F32), ((C * ROWS, N), BF16), (fwd_high.shap...  2.71 us
    pallas_call x1, Pallas kernels, on_device(): call(prepare, [((N, N), F32), (along_high.shape, BF16), (along_low.shape,...  1.7 us
  transfers between devices with their start and end apart: 1, of which 1 were waited for; matrix products, arithmetic and copies ran while one was open for 0% of the time, Pallas kernels for 2%

profile of v6, /device:TPU:1, one launch (start us, length us, event | category | flops | bytes accessed | tf_op | source)
XLA Modules:
  0.0 83.7 jit_solution(6679036393270875251)
XLA Ops:
  0.6 2.7 %shard_map.113 = (f32[128,128]{1,0:T(8,128)}, bf16[4096,256]{1,0:T(8,128)(2,1)S(1)}, bf16[256,256]{1,0:T(8,128)(2,1)S(1)}, bf16[256,256]{1,0:T(8,128)(2,1)S(1)}) custom-call(f32[64]{0:T(128)} %weight_hbm.1, bf16[64,256]{1,0:T(8,128)(2,1)} %bitcast.17, bf16[4096,256]{1,0:T(8,128)(2,1)} %bitcast.16, bf16[256,256]{1,0:T(8,128)(2,1)} %constant.12.clone.high_hbm, ...), custom_call_target="tpu_custom_call" | custom-call | flops 200000000 | bytes 3000000 | tf_op jit(solution)/shard_map/pallas_call | solution.py:240
  3.4 7.4 %all-to-all-start = ((f32[8,16,128]{2,1,0:T(8,128)}), f32[8,16,128]{2,1,0:T(8,128)S(1)}, u32[]{:S(2)}, u32[]{:S(2)}) async-start(f32[8,16,128]{2,1,0:T(8,128)} %bitcast.2), calls=%async_computation | async-start | bytes 131072 | tf_op jit(solution)/shard_map/all_to_all | solution.py:255
  11.4 1.7 %shard_map.114 = (f32[256,256]{1,0:T(8,128)S(1)}, bf16[512,256]{1,0:T(8,128)(2,1)S(1)}, bf16[512,256]{1,0:T(8,128)(2,1)S(1)}) custom-call(s32[1]{0:T(128)S(6)} %copy.16.turn, s32[2,8]{1,0:T(2,128)} %bitcast.19, s32[256,256]{1,0:T(8,128)} %wedge_hbm.1, bf16[512,256]{1,0:T(8,128)(2,1)} %constant.14.clone.high_hbm, bf16[512,256]{1,0:T(8,128)(2,1)} %constant.15.clone.low_hbm), custom_call_target="tpu_custom_call" | custom-call | flops 200000000 | bytes 3000000 | tf_op jit(solution)/shard_map/pallas_call | solution.py:248
  13.1 3.4 %all-to-all-done = f32[8,16,128]{2,1,0:T(8,128)S(1)} async-done(((f32[8,16,128]{2,1,0:T(8,128)}), f32[8,16,128]{2,1,0:T(8,128)S(1)}, u32[]{:S(2)}, u32[]{:S(2)}) %all-to-all-start) | async-done | bytes 65568 | tf_op jit(solution)/shard_map/all_to_all | solution.py:255
  16.5 1.3 %shard_map.115 = f32[512,128]{1,0:T(8,128)S(1)} custom-call(f32[128,128]{1,0:T(8,128)S(1)} %bitcast.14, f32[256,256]{1,0:T(8,128)S(1)} %get-tuple-element.16.factors, bf16[512,256]{1,0:T(8,128)(2,1)S(1)} %get-tuple-element.17.along_high, bf16[512,256]{1,0:T(8,128)(2,1)S(1)} %get-tuple-element.18.along_low), custom_call_target="tpu_custom_call" | custom-call | flops 200000000 | bytes 2000000 | tf_op jit(solution)/shard_map/pallas_call | solution.py:256
  17.8 31.0 %all_to_all.20 = f32[32,16,128]{2,1,0:T(8,128)S(1)} all-to-all(f32[32,16,128]{2,1,0:T(8,128)S(1)} %bitcast.13), channel_id=1, replica_groups=mesh['y'=4,'xh'=2,'core'=2,'zh'=4,'zl'=4,'xl'=2] {'zh','zl','xl'}, dimensions={0} | all-to-all | bytes 524288 | tf_op jit(solution)/shard_map/all_to_all | solution.py:259
  48.8 1.0 %shard_map.116 = (f32[64,256]{1,0:T(8,128)}, f32[64,128]{1,0:T(8,128)S(1)}) custom-call(f32[512,128]{1,0:T(8,128)S(1)} %bitcast.12, bf16[4096,256]{1,0:T(8,128)(2,1)S(1)} %get-tuple-element.19.features, bf16[256,256]{1,0:T(8,128)(2,1)S(1)} %get-tuple-element.20.fwd_high, bf16[256,256]{1,0:T(8,128)(2,1)S(1)} %get-tuple-element.21.fwd_low), custom_call_target="tpu_custom_call" | custom-call | flops 200000000 | bytes 3000000 | tf_op jit(solution)/shard_map/pallas_call | solution.py:262
  49.8 20.6 %all_to_all.21 = f32[64,1,128]{2,1,0:T(1,128)S(1)} all-to-all(f32[64,1,128]{2,1,0:T(1,128)S(1)} %bitcast.15), channel_id=1, replica_groups=mesh['y'=4,'xh'=2,'core'=2,'zh'=4,'zl'=4,'xl'=2] {'core','zh','zl','xl'}, dimensions={0} | all-to-all | bytes 65536 | tf_op jit(solution)/shard_map/all_to_all | solution.py:269
  70.4 0.1 reduce_sum.18
  70.5 12.7 %all_to_all.22 = f32[8,1,128]{2,1,0:T(1,128)S(1)} all-to-all(f32[8,1,128]{2,1,0:T(1,128)S(1)} %broadcast_in_dim.2), channel_id=1, replica_groups=mesh['y'=4,'xh'=2,'core'=2,'zh'=4,'zl'=4,'xl'=2] {'y','xh'}, dimensions={0} | all-to-all | bytes 8192 | tf_op jit(solution)/shard_map/all_to_all | solution.py:272
  83.2 0.5 slice_multiply_fusion
  (2 shorter events, 0.0 us)
Async XLA Ops:
  3.4 13.1 %all-to-all-start = ((f32[8,16,128]{2,1,0:T(8,128)}), f32[8,16,128]{2,1,0:T(8,128)S(1)}, u32[]{:S(2)}, u32[]{:S(2)}) async-start(f32[8,16,128]{2,1,0:T(8,128)} %bitcast.2), calls=%async_computation | async-start | bytes 131072 | tf_op jit(solution)/shard_map/all_to_all | solution.py:255

commit v7 on v5

--- a/solution.py
+++ b/solution.py
@@ -22,6 +22,9 @@
 PARTS = {"dp": (("y", 4), ("xh", 2), ("core", 2)), "slab": (("z", 16), ("xl", 2))}
 NEAR = ("y", "xh")
 FAR = ("core", "z", "xl")
+HALF = SLABS // 2
+FIRST_FAR = 17
+FIRST_NEAR = 5
 
 F32, BF16 = jnp.float32, jnp.bfloat16
 VMEM_LIMIT = 16 * 1024 * 1024
@@ -37,12 +40,12 @@
     step = 2.0 * math.pi / N
     space = np.arange(N)
     quad, slab = np.meshgrid(np.arange(4), np.arange(SLABS), indexing="ij")
-    freq = (4 * slab + quad).reshape(-1)
+    freq = (4 * ((slab + HALF) % SLABS) + quad).reshape(-1)
     phase = (freq[:, None] * space[None, :]) % N * step
     real, imag = np.cos(phase), -np.sin(phase)
     imag[freq == 0] = np.cos(math.pi * space)
     zp, m, i = np.meshgrid(np.arange(2), np.arange(4), np.arange(SLABS), indexing="ij")
-    depth = (8 * i + 2 * m + zp).reshape(-1)
+    depth = (8 * ((i + HALF) % SLABS) + 2 * m + zp).reshape(-1)
     phase = (depth[:, None] * depth[None, :]) % N * step
     along = np.concatenate([np.cos(phase), np.sin(phase)], 0)
     return halves(np.concatenate([real, imag], 0)) + halves(along)
@@ -98,7 +101,7 @@
     direct = jnp.where(odd, other[:, 128:], plain[:, :128])
     mirror = jnp.where(odd, other[:, :128], plain[:, 128:]).astype(BF16)
     r = lax.broadcasted_iota(jnp.int32, (N, N), 0)
-    p = 8 * (r & 31) + 2 * ((r >> 5) & 3) + (r >> 7)
+    p = (8 * ((r & 31) + HALF) + 2 * ((r >> 5) & 3) + (r >> 7)) & (N - 1)
     k = lane_of((N, N))
     keep = (k == p).astype(F32).astype(BF16)
     flip = (((p + k) & (N - 1)) == 0).astype(F32).astype(BF16)
@@ -175,7 +178,7 @@
     blocks = [lines[pl.ds(m, SLABS, stride=4), :] for m in range(4)]
     line = jnp.concatenate([regroup(blocks, q) for q in range(4)], 0).T
     line = jnp.concatenate([line[:64], line[64:]], 1)
-    line = line * jnp.where((lane_of((ROWS, N)) & 127) == 0, 1.0 / (N * N), 2.0 / (N * N))
+    line = line * jnp.where((lane_of((ROWS, N)) & 127) == HALF, 1.0 / (N * N), 2.0 / (N * N))
     high, low = split(line)
     both = dot(jnp.concatenate([high, low], 0), fwd_high[...])
     values = both[:ROWS] + (both[ROWS:] + dot(high, fwd_low[...]))
@@ -214,6 +217,11 @@
         compiler_params=pltpu.CompilerParams(vmem_limit_bytes=VMEM_LIMIT),
         cost_estimate=pl.CostEstimate(flops=cost[0], bytes_accessed=cost[1], transcendentals=0),
     )
+
+
+def exchange(array, names, size, first):
+    order = [[(first + n) % size for n in range(size)]]
+    return lax.all_to_all(array, names, 0, 0, axis_index_groups=order, tiled=True)
 
 
 def hbm(array):
@@ -240,11 +248,11 @@
         [pltpu.SMEM((2, NB), jnp.int32), pltpu.VMEM((N, N), jnp.int32), pltpu.SemaphoreType.DMA((4,))],
         (200_000_000, 3_000_000),
     )(rotation, hbm(blocks.T), hbm(wedge), along_high, along_low)
-    lines = lax.all_to_all(lines.reshape(SLABS, 4, 128), slab, 0, 0, tiled=True).reshape(128, 128)
+    lines = exchange(lines.reshape(SLABS, 4, 128), slab, SLABS, HALF).reshape(128, 128)
     (back,) = call(filter_z, [((128, 128), F32)], "vvvv>v", (), (200_000_000, 2_000_000))(
         lines, factors, along_high, along_low
     )
-    back = lax.all_to_all(back.reshape(SLABS, 4, 128), slab, 0, 0, tiled=True).reshape(128, 128)
+    back = exchange(back.reshape(SLABS, 4, 128), slab, SLABS, HALF).reshape(128, 128)
     far = math.prod(sizes[name] for name in FAR)
     near = math.prod(sizes[name] for name in NEAR)
     volume, sums = call(
@@ -254,10 +262,10 @@
         [pltpu.VMEM((ROWS, N), F32), pltpu.VMEM((C * YP, 128), F32), pltpu.SemaphoreType.DMA],
         (200_000_000, 3_000_000),
     )(back, features, fwd_high, fwd_low)
-    sums = lax.all_to_all(sums.reshape(far, 1, 128), FAR, 0, 0, tiled=True)
+    sums = exchange(sums.reshape(far, 1, 128), FAR, far, FIRST_FAR % far)
     sums = jnp.sum(sums, 0, keepdims=True)
     sums = jnp.broadcast_to(sums, (near, 1, 128))
-    sums = lax.all_to_all(sums, NEAR, 0, 0, tiled=True)
+    sums = exchange(sums, NEAR, near, FIRST_NEAR % near)
     w_grad = jnp.sum(sums, (0, 1))[:C] * (1.0 / (math.prod(sizes.values()) * ROWS * N))
     return volume.reshape(1, ZL, YP, N), w_grad
 

time: 83.5 us -> 74.6 us (0.89)
  the two profiles are of different devices: /device:TPU:1 before, /device:TPU:6 now
where the time goes in v7:
time: 74.6 us; the launch traced here: 74.3 us
  blocking collectives  45 us (60%)
  starting transfers between devices  19.9 us (27%)
  Pallas kernels  5.99 us (8%)
  waiting for transfers between devices  1.44 us (2%)
  between operations  1.32 us (2%)
    all_to_all x3, blocking collectives, exchange(): lax.all_to_all(array, names, 0, 0, axis_index_groups=order, tiled=True)  45 us
    all_to_all x1, starting transfers between devices, exchange(): lax.all_to_all(array, names, 0, 0, axis_index_groups=order, tiled=True)  19.9 us
    pallas_call x1, Pallas kernels, on_device(): call(forward_x, [((128, 128), F32), ((C * ROWS, N), BF16), (fwd_high.shap...  2.71 us
  transfers between devices with their start and end apart: 1, of which 1 were waited for; matrix products, arithmetic and copies ran while one was open for 0% of the time, Pallas kernels for 2%

profile of v7, /device:TPU:6, one launch (start us, length us, event | category | flops | bytes accessed | tf_op | source)
XLA Modules:
  0.0 74.3 jit_solution(941760969996995219)
XLA Ops:
  0.6 2.7 %shard_map.113 = (f32[128,128]{1,0:T(8,128)}, bf16[4096,256]{1,0:T(8,128)(2,1)S(1)}, bf16[256,256]{1,0:T(8,128)(2,1)S(1)}, bf16[256,256]{1,0:T(8,128)(2,1)S(1)}) custom-call(f32[64]{0:T(128)} %weight_hbm.1, bf16[64,256]{1,0:T(8,128)(2,1)} %bitcast.17, bf16[4096,256]{1,0:T(8,128)(2,1)} %bitcast.16, bf16[256,256]{1,0:T(8,128)(2,1)} %constant.12.clone.high_hbm, ...), custom_call_target="tpu_custom_call" | custom-call | flops 200000000 | bytes 3000000 | tf_op jit(solution)/shard_map/pallas_call | solution.py:236
  3.3 19.9 %all-to-all-start = ((f32[32,4,128]{2,1,0:T(4,128)}), f32[32,4,128]{2,1,0:T(4,128)S(1)}, u32[]{:S(2)}, u32[]{:S(2)}) async-start(f32[32,4,128]{2,1,0:T(4,128)} %bitcast.2), calls=%async_computation | async-start | bytes 131072 | tf_op jit(solution)/shard_map/all_to_all | solution.py:224
  23.9 1.5 %shard_map.114 = (f32[256,128]{1,0:T(8,128)S(1)}, bf16[512,256]{1,0:T(8,128)(2,1)S(1)}, bf16[512,256]{1,0:T(8,128)(2,1)S(1)}) custom-call(s32[1]{0:T(128)S(6)} %copy.16.turn, s32[2,8]{1,0:T(2,128)} %bitcast.19, s32[256,256]{1,0:T(8,128)} %wedge_hbm.1, bf16[512,256]{1,0:T(8,128)(2,1)} %constant.14.clone.high_hbm, bf16[512,256]{1,0:T(8,128)(2,1)} %constant.15.clone.low_hbm), custom_call_target="tpu_custom_call" | custom-call | flops 200000000 | bytes 3000000 | tf_op jit(solution)/shard_map/pallas_call | solution.py:244
  25.4 1.4 %all-to-all-done = f32[32,4,128]{2,1,0:T(4,128)S(1)} async-done(((f32[32,4,128]{2,1,0:T(4,128)}), f32[32,4,128]{2,1,0:T(4,128)S(1)}, u32[]{:S(2)}, u32[]{:S(2)}) %all-to-all-start) | async-done | bytes 65568 | tf_op jit(solution)/shard_map/all_to_all | solution.py:224
  26.8 0.8 %shard_map.115 = f32[128,128]{1,0:T(8,128)S(1)} custom-call(f32[128,128]{1,0:T(8,128)S(1)} %bitcast.12, f32[256,128]{1,0:T(8,128)S(1)} %get-tuple-element.16.factors, bf16[512,256]{1,0:T(8,128)(2,1)S(1)} %get-tuple-element.17.along_high, bf16[512,256]{1,0:T(8,128)(2,1)S(1)} %get-tuple-element.18.along_low), custom_call_target="tpu_custom_call" | custom-call | flops 200000000 | bytes 2000000 | tf_op jit(solution)/shard_map/pallas_call | solution.py:252
  27.6 16.6 %all_to_all.20 = f32[32,4,128]{2,1,0:T(4,128)S(1)} all-to-all(f32[32,4,128]{2,1,0:T(4,128)S(1)} %bitcast.14), channel_id=1, replica_groups={{16,17,18,19,20,21,22,23,24,25,26,27,28,29,30,31,0,1,2,3,4,5,6,7,8,9,10..., dimensions={0} | all-to-all | bytes 131072 | tf_op jit(solution)/shard_map/all_to_all | solution.py:224
  44.3 1.0 %shard_map.116 = (f32[64,256]{1,0:T(8,128)}, f32[64,128]{1,0:T(8,128)S(1)}) custom-call(f32[128,128]{1,0:T(8,128)S(1)} %bitcast.13, bf16[4096,256]{1,0:T(8,128)(2,1)S(1)} %get-tuple-element.19.features, bf16[256,256]{1,0:T(8,128)(2,1)S(1)} %get-tuple-element.20.fwd_high, bf16[256,256]{1,0:T(8,128)(2,1)S(1)} %get-tuple-element.21.fwd_low), custom_call_target="tpu_custom_call" | custom-call | flops 200000000 | bytes 3000000 | tf_op jit(solution)/shard_map/pallas_call | solution.py:258
  45.3 17.3 %all_to_all.21 = f32[64,1,128]{2,1,0:T(1,128)S(1)} all-to-all(f32[64,1,128]{2,1,0:T(1,128)S(1)} %bitcast.15), channel_id=1, replica_groups={{17,18,19,20,21,22,23,24,25,26,27,28,29,30,31,32,33,34,35,36,37,38,39,4..., dimensions={0} | all-to-all | bytes 65536 | tf_op jit(solution)/shard_map/all_to_all | solution.py:224
  62.6 0.1 reduce_sum.18
  62.7 11.1 %all_to_all.22 = f32[8,1,128]{2,1,0:T(1,128)S(1)} all-to-all(f32[8,1,128]{2,1,0:T(1,128)S(1)} %broadcast_in_dim.2), channel_id=1, replica_groups={{320,384,448,0,64,128,192,256},{321,385,449,1,65,129,193,257},{322,386,..., dimensions={0} | all-to-all | bytes 8192 | tf_op jit(solution)/shard_map/all_to_all | solution.py:224
  73.8 0.5 slice_multiply_fusion
  (2 shorter events, 0.0 us)
Async XLA Ops:
  3.3 23.5 %all-to-all-start = ((f32[32,4,128]{2,1,0:T(4,128)}), f32[32,4,128]{2,1,0:T(4,128)S(1)}, u32[]{:S(2)}, u32[]{:S(2)}) async-start(f32[32,4,128]{2,1,0:T(4,128)} %bitcast.2), calls=%async_computation | async-start | bytes 131072 | tf_op jit(solution)/shard_map/all_to_all | solution.py:224

commit v8 on v7

--- a/solution.py
+++ b/solution.py
@@ -20,11 +20,11 @@
 ROWS = ZL * YP
 CHUNKS = 8
 PARTS = {"dp": (("y", 4), ("xh", 2), ("core", 2)), "slab": (("z", 16), ("xl", 2))}
-NEAR = ("y", "xh")
-FAR = ("core", "z", "xl")
+NEAR = ("y", "xh", "xl")
+FAR = ("core", "z")
 HALF = SLABS // 2
-FIRST_FAR = 17
-FIRST_NEAR = 5
+FIRST_FAR = 8
+FIRST_NEAR = 10
 
 F32, BF16 = jnp.float32, jnp.bfloat16
 VMEM_LIMIT = 16 * 1024 * 1024

time: 74.6 us -> 72.5 us (0.972)
  the two profiles are of different devices: /device:TPU:6 before, /device:TPU:1 now
where the time goes in v8:
time: 72.5 us; the launch traced here: 71.7 us
  blocking collectives  41.8 us (58%)
  starting transfers between devices  20.2 us (28%)
  Pallas kernels  6 us (8%)
  waiting for transfers between devices  1.77 us (2%)
  between operations  1.32 us (2%)
    all_to_all x3, blocking collectives, exchange(): lax.all_to_all(array, names, 0, 0, axis_index_groups=order, tiled=True)  41.8 us
    all_to_all x1, starting transfers between devices, exchange(): lax.all_to_all(array, names, 0, 0, axis_index_groups=order, tiled=True)  20.2 us
    pallas_call x1, Pallas kernels, on_device(): call(forward_x, [((128, 128), F32), ((C * ROWS, N), BF16), (fwd_high.shap...  2.71 us
    all_to_all x1, waiting for transfers between devices, exchange(): lax.all_to_all(array, names, 0, 0, axis_index_groups=order, tiled=True)  1.77 us
    pallas_call x1, Pallas kernels, on_device(): call(prepare, [((N, 128), F32), (along_high.shape, BF16), (along_low.shap...  1.48 us
  transfers between devices with their start and end apart: 1, of which 1 were waited for; matrix products, arithmetic and copies ran while one was open for 0% of the time, Pallas kernels for 2%

profile of v8, /device:TPU:1, one launch (start us, length us, event | category | flops | bytes accessed | tf_op | source)
XLA Modules:
  0.0 71.7 jit_solution(4226822168973845830)
XLA Ops:
  0.6 2.7 %shard_map.113 = (f32[128,128]{1,0:T(8,128)}, bf16[4096,256]{1,0:T(8,128)(2,1)S(1)}, bf16[256,256]{1,0:T(8,128)(2,1)S(1)}, bf16[256,256]{1,0:T(8,128)(2,1)S(1)}) custom-call(f32[64]{0:T(128)} %weight_hbm.1, bf16[64,256]{1,0:T(8,128)(2,1)} %bitcast.18, bf16[4096,256]{1,0:T(8,128)(2,1)} %bitcast.16, bf16[256,256]{1,0:T(8,128)(2,1)} %constant.12.clone.high_hbm, ...), custom_call_target="tpu_custom_call" | custom-call | flops 200000000 | bytes 3000000 | tf_op jit(solution)/shard_map/pallas_call | solution.py:236
  3.4 20.2 %all-to-all-start = ((f32[32,4,128]{2,1,0:T(4,128)}), f32[32,4,128]{2,1,0:T(4,128)S(1)}, u32[]{:S(2)}, u32[]{:S(2)}) async-start(f32[32,4,128]{2,1,0:T(4,128)} %bitcast.2), calls=%async_computation | async-start | bytes 131072 | tf_op jit(solution)/shard_map/all_to_all | solution.py:224
  24.2 1.5 %shard_map.114 = (f32[256,128]{1,0:T(8,128)S(1)}, bf16[512,256]{1,0:T(8,128)(2,1)S(1)}, bf16[512,256]{1,0:T(8,128)(2,1)S(1)}) custom-call(s32[1]{0:T(128)S(6)} %copy.16.turn, s32[2,8]{1,0:T(2,128)} %bitcast.19, s32[256,256]{1,0:T(8,128)} %wedge_hbm.1, bf16[512,256]{1,0:T(8,128)(2,1)} %constant.14.clone.high_hbm, bf16[512,256]{1,0:T(8,128)(2,1)} %constant.15.clone.low_hbm), custom_call_target="tpu_custom_call" | custom-call | flops 200000000 | bytes 3000000 | tf_op jit(solution)/shard_map/pallas_call | solution.py:244
  25.7 1.8 %all-to-all-done = f32[32,4,128]{2,1,0:T(4,128)S(1)} async-done(((f32[32,4,128]{2,1,0:T(4,128)}), f32[32,4,128]{2,1,0:T(4,128)S(1)}, u32[]{:S(2)}, u32[]{:S(2)}) %all-to-all-start) | async-done | bytes 65568 | tf_op jit(solution)/shard_map/all_to_all | solution.py:224
  27.5 0.8 %shard_map.115 = f32[128,128]{1,0:T(8,128)S(1)} custom-call(f32[128,128]{1,0:T(8,128)S(1)} %bitcast.12, f32[256,128]{1,0:T(8,128)S(1)} %get-tuple-element.16.factors, bf16[512,256]{1,0:T(8,128)(2,1)S(1)} %get-tuple-element.17.along_high, bf16[512,256]{1,0:T(8,128)(2,1)S(1)} %get-tuple-element.18.along_low), custom_call_target="tpu_custom_call" | custom-call | flops 200000000 | bytes 2000000 | tf_op jit(solution)/shard_map/pallas_call | solution.py:252
  28.2 15.5 %all_to_all.20 = f32[32,4,128]{2,1,0:T(4,128)S(1)} all-to-all(f32[32,4,128]{2,1,0:T(4,128)S(1)} %bitcast.14), channel_id=1, replica_groups={{16,17,18,19,20,21,22,23,24,25,26,27,28,29,30,31,0,1,2,3,4,5,6,7,8,9,10..., dimensions={0} | all-to-all | bytes 131072 | tf_op jit(solution)/shard_map/all_to_all | solution.py:224
  43.8 1.0 %shard_map.116 = (f32[64,256]{1,0:T(8,128)}, f32[32,128]{1,0:T(8,128)S(1)}) custom-call(f32[128,128]{1,0:T(8,128)S(1)} %bitcast.13, bf16[4096,256]{1,0:T(8,128)(2,1)S(1)} %get-tuple-element.19.features, bf16[256,256]{1,0:T(8,128)(2,1)S(1)} %get-tuple-element.20.fwd_high, bf16[256,256]{1,0:T(8,128)(2,1)S(1)} %get-tuple-element.21.fwd_low), custom_call_target="tpu_custom_call" | custom-call | flops 200000000 | bytes 3000000 | tf_op jit(solution)/shard_map/pallas_call | solution.py:258
  44.8 17.0 %all_to_all.21 = f32[32,1,128]{2,1,0:T(1,128)S(1)} all-to-all(f32[32,1,128]{2,1,0:T(1,128)S(1)} %bitcast.15), channel_id=1, replica_groups={{16,18,20,22,24,26,28,30,32,34,36,38,40,42,44,46,48,50,52,54,56,58,60,6..., dimensions={0} | all-to-all | bytes 32768 | tf_op jit(solution)/shard_map/all_to_all | solution.py:224
  61.8 0.1 reduce_sum.18
  61.9 9.3 %all_to_all.22 = f32[16,1,128]{2,1,0:T(1,128)S(1)} all-to-all(f32[16,1,128]{2,1,0:T(1,128)S(1)} %broadcast_in_dim.2), channel_id=1, replica_groups={{320,321,384,385,448,449,0,1,64,65,128,129,192,193,256,257},{322,323,38..., dimensions={0} | all-to-all | bytes 16384 | tf_op jit(solution)/shard_map/all_to_all | solution.py:224
  71.2 0.5 slice_multiply_fusion
  (2 shorter events, 0.0 us)
Async XLA Ops:
  3.4 24.1 %all-to-all-start = ((f32[32,4,128]{2,1,0:T(4,128)}), f32[32,4,128]{2,1,0:T(4,128)S(1)}, u32[]{:S(2)}, u32[]{:S(2)}) async-start(f32[32,4,128]{2,1,0:T(4,128)} %bitcast.2), calls=%async_computation | async-start | bytes 131072 | tf_op jit(solution)/shard_map/all_to_all | solution.py:224

commit v9 on v8

--- a/solution.py
+++ b/solution.py
@@ -20,11 +20,11 @@
 ROWS = ZL * YP
 CHUNKS = 8
 PARTS = {"dp": (("y", 4), ("xh", 2), ("core", 2)), "slab": (("z", 16), ("xl", 2))}
-NEAR = ("y", "xh", "xl")
-FAR = ("core", "z")
+NEAR = ("y", "xh", "xl", "core")
+FAR = ("z",)
 HALF = SLABS // 2
 FIRST_FAR = 8
-FIRST_NEAR = 10
+FIRST_NEAR = 20
 
 F32, BF16 = jnp.float32, jnp.bfloat16
 VMEM_LIMIT = 16 * 1024 * 1024

time: 72.5 us -> 73.1 us (level)
  blocking collectives: 41.8 us -> 42.9 us
    all_to_all x3, blocking collectives: 41.8 us -> 42.9 us  [exchange(): lax.all_to_all(array, names, 0, 0, axis_index_groups=order, tiled=True)]
where the time goes in v9:
time: 73.1 us; the launch traced here: 72.8 us
  blocking collectives  42.9 us (59%)
  starting transfers between devices  20.2 us (28%)
  Pallas kernels  5.99 us (8%)
  waiting for transfers between devices  1.77 us (2%)
  between operations  1.32 us (2%)
    all_to_all x3, blocking collectives, exchange(): lax.all_to_all(array, names, 0, 0, axis_index_groups=order, tiled=True)  42.9 us
    all_to_all x1, starting transfers between devices, exchange(): lax.all_to_all(array, names, 0, 0, axis_index_groups=order, tiled=True)  20.2 us
    pallas_call x1, Pallas kernels, on_device(): call(forward_x, [((128, 128), F32), ((C * ROWS, N), BF16), (fwd_high.shap...  2.71 us
    all_to_all x1, waiting for transfers between devices, exchange(): lax.all_to_all(array, names, 0, 0, axis_index_groups=order, tiled=True)  1.77 us
    pallas_call x1, Pallas kernels, on_device(): call(prepare, [((N, 128), F32), (along_high.shape, BF16), (along_low.shap...  1.48 us
  transfers between devices with their start and end apart: 1, of which 1 were waited for; matrix products, arithmetic and copies ran while one was open for 0% of the time, Pallas kernels for 2%

profile of v9, /device:TPU:1, one launch (start us, length us, event | category | flops | bytes accessed | tf_op | source)
XLA Modules:
  0.0 72.8 jit_solution(12748494174283803068)
XLA Ops:
  0.6 2.7 %shard_map.113 = (f32[128,128]{1,0:T(8,128)}, bf16[4096,256]{1,0:T(8,128)(2,1)S(1)}, bf16[256,256]{1,0:T(8,128)(2,1)S(1)}, bf16[256,256]{1,0:T(8,128)(2,1)S(1)}) custom-call(f32[64]{0:T(128)} %weight_hbm.1, bf16[64,256]{1,0:T(8,128)(2,1)} %bitcast.18, bf16[4096,256]{1,0:T(8,128)(2,1)} %bitcast.16, bf16[256,256]{1,0:T(8,128)(2,1)} %constant.12.clone.high_hbm, ...), custom_call_target="tpu_custom_call" | custom-call | flops 200000000 | bytes 3000000 | tf_op jit(solution)/shard_map/pallas_call | solution.py:236
  3.4 20.2 %all-to-all-start = ((f32[32,4,128]{2,1,0:T(4,128)}), f32[32,4,128]{2,1,0:T(4,128)S(1)}, u32[]{:S(2)}, u32[]{:S(2)}) async-start(f32[32,4,128]{2,1,0:T(4,128)} %bitcast.2), calls=%async_computation | async-start | bytes 131072 | tf_op jit(solution)/shard_map/all_to_all | solution.py:224
  24.2 1.5 %shard_map.114 = (f32[256,128]{1,0:T(8,128)S(1)}, bf16[512,256]{1,0:T(8,128)(2,1)S(1)}, bf16[512,256]{1,0:T(8,128)(2,1)S(1)}) custom-call(s32[1]{0:T(128)S(6)} %copy.16.turn, s32[2,8]{1,0:T(2,128)} %bitcast.19, s32[256,256]{1,0:T(8,128)} %wedge_hbm.1, bf16[512,256]{1,0:T(8,128)(2,1)} %constant.14.clone.high_hbm, bf16[512,256]{1,0:T(8,128)(2,1)} %constant.15.clone.low_hbm), custom_call_target="tpu_custom_call" | custom-call | flops 200000000 | bytes 3000000 | tf_op jit(solution)/shard_map/pallas_call | solution.py:244
  25.7 1.8 %all-to-all-done = f32[32,4,128]{2,1,0:T(4,128)S(1)} async-done(((f32[32,4,128]{2,1,0:T(4,128)}), f32[32,4,128]{2,1,0:T(4,128)S(1)}, u32[]{:S(2)}, u32[]{:S(2)}) %all-to-all-start) | async-done | bytes 65568 | tf_op jit(solution)/shard_map/all_to_all | solution.py:224
  27.5 0.8 %shard_map.115 = f32[128,128]{1,0:T(8,128)S(1)} custom-call(f32[128,128]{1,0:T(8,128)S(1)} %bitcast.12, f32[256,128]{1,0:T(8,128)S(1)} %get-tuple-element.16.factors, bf16[512,256]{1,0:T(8,128)(2,1)S(1)} %get-tuple-element.17.along_high, bf16[512,256]{1,0:T(8,128)(2,1)S(1)} %get-tuple-element.18.along_low), custom_call_target="tpu_custom_call" | custom-call | flops 200000000 | bytes 2000000 | tf_op jit(solution)/shard_map/pallas_call | solution.py:252
  28.2 15.5 %all_to_all.20 = f32[32,4,128]{2,1,0:T(4,128)S(1)} all-to-all(f32[32,4,128]{2,1,0:T(4,128)S(1)} %bitcast.14), channel_id=1, replica_groups={{16,17,18,19,20,21,22,23,24,25,26,27,28,29,30,31,0,1,2,3,4,5,6,7,8,9,10..., dimensions={0} | all-to-all | bytes 131072 | tf_op jit(solution)/shard_map/all_to_all | solution.py:224
  43.8 1.0 %shard_map.116 = (f32[64,256]{1,0:T(8,128)}, f32[16,128]{1,0:T(8,128)S(1)}) custom-call(f32[128,128]{1,0:T(8,128)S(1)} %bitcast.13, bf16[4096,256]{1,0:T(8,128)(2,1)S(1)} %get-tuple-element.19.features, bf16[256,256]{1,0:T(8,128)(2,1)S(1)} %get-tuple-element.20.fwd_high, bf16[256,256]{1,0:T(8,128)(2,1)S(1)} %get-tuple-element.21.fwd_low), custom_call_target="tpu_custom_call" | custom-call | flops 200000000 | bytes 3000000 | tf_op jit(solution)/shard_map/pallas_call | solution.py:258
  44.8 12.9 %all_to_all.21 = f32[16,1,128]{2,1,0:T(1,128)S(1)} all-to-all(f32[16,1,128]{2,1,0:T(1,128)S(1)} %bitcast.15), channel_id=1, replica_groups={{16,18,20,22,24,26,28,30,0,2,4,6,8,10,12,14},{17,19,21,23,25,27,29,31,1..., dimensions={0} | all-to-all | bytes 16384 | tf_op jit(solution)/shard_map/all_to_all | solution.py:224
  57.8 14.5 %all_to_all.22 = f32[32,1,128]{2,1,0:T(1,128)S(1)} all-to-all(f32[32,1,128]{2,1,0:T(1,128)S(1)} %broadcast_in_dim.2), channel_id=1, replica_groups={{320,352,321,353,384,416,385,417,448,480,449,481,0,32,1,33,64,96,65,97,..., dimensions={0} | all-to-all | bytes 32768 | tf_op jit(solution)/shard_map/all_to_all | solution.py:224
  72.3 0.5 slice_multiply_fusion
  (3 shorter events, 0.1 us)
Async XLA Ops:
  3.4 24.1 %all-to-all-start = ((f32[32,4,128]{2,1,0:T(4,128)}), f32[32,4,128]{2,1,0:T(4,128)S(1)}, u32[]{:S(2)}, u32[]{:S(2)}) async-start(f32[32,4,128]{2,1,0:T(4,128)} %bitcast.2), calls=%async_computation | async-start | bytes 131072 | tf_op jit(solution)/shard_map/all_to_all | solution.py:224

commit v10 on v8

--- a/solution.py
+++ b/solution.py
@@ -23,7 +23,7 @@
 NEAR = ("y", "xh", "xl")
 FAR = ("core", "z")
 HALF = SLABS // 2
-FIRST_FAR = 8
+FIRST_FAR = 24
 FIRST_NEAR = 10
 
 F32, BF16 = jnp.float32, jnp.bfloat16

time: 72.5 us -> 71.7 us (0.989)
  blocking collectives: 41.8 us -> 41 us
    all_to_all x3, blocking collectives: 41.8 us -> 41 us  [exchange(): lax.all_to_all(array, names, 0, 0, axis_index_groups=order, tiled=True)]
where the time goes in v10:
time: 71.7 us; the launch traced here: 70.8 us
  blocking collectives  41 us (57%)
  starting transfers between devices  20.2 us (28%)
  Pallas kernels  6 us (8%)
  waiting for transfers between devices  1.77 us (2%)
  between operations  1.32 us (2%)
    all_to_all x3, blocking collectives, exchange(): lax.all_to_all(array, names, 0, 0, axis_index_groups=order, tiled=True)  41 us
    all_to_all x1, starting transfers between devices, exchange(): lax.all_to_all(array, names, 0, 0, axis_index_groups=order, tiled=True)  20.2 us
    pallas_call x1, Pallas kernels, on_device(): call(forward_x, [((128, 128), F32), ((C * ROWS, N), BF16), (fwd_high.shap...  2.71 us
    all_to_all x1, waiting for transfers between devices, exchange(): lax.all_to_all(array, names, 0, 0, axis_index_groups=order, tiled=True)  1.77 us
    pallas_call x1, Pallas kernels, on_device(): call(prepare, [((N, 128), F32), (along_high.shape, BF16), (along_low.shap...  1.48 us
  transfers between devices with their start and end apart: 1, of which 1 were waited for; matrix products, arithmetic and copies ran while one was open for 0% of the time, Pallas kernels for 2%

profile of v10, /device:TPU:1, one launch (start us, length us, event | category | flops | bytes accessed | tf_op | source)
XLA Modules:
  0.0 70.8 jit_solution(5903925645308651254)
XLA Ops:
  0.6 2.7 %shard_map.113 = (f32[128,128]{1,0:T(8,128)}, bf16[4096,256]{1,0:T(8,128)(2,1)S(1)}, bf16[256,256]{1,0:T(8,128)(2,1)S(1)}, bf16[256,256]{1,0:T(8,128)(2,1)S(1)}) custom-call(f32[64]{0:T(128)} %weight_hbm.1, bf16[64,256]{1,0:T(8,128)(2,1)} %bitcast.18, bf16[4096,256]{1,0:T(8,128)(2,1)} %bitcast.16, bf16[256,256]{1,0:T(8,128)(2,1)} %constant.12.clone.high_hbm, ...), custom_call_target="tpu_custom_call" | custom-call | flops 200000000 | bytes 3000000 | tf_op jit(solution)/shard_map/pallas_call | solution.py:236
  3.4 20.2 %all-to-all-start = ((f32[32,4,128]{2,1,0:T(4,128)}), f32[32,4,128]{2,1,0:T(4,128)S(1)}, u32[]{:S(2)}, u32[]{:S(2)}) async-start(f32[32,4,128]{2,1,0:T(4,128)} %bitcast.2), calls=%async_computation | async-start | bytes 131072 | tf_op jit(solution)/shard_map/all_to_all | solution.py:224
  24.2 1.5 %shard_map.114 = (f32[256,128]{1,0:T(8,128)S(1)}, bf16[512,256]{1,0:T(8,128)(2,1)S(1)}, bf16[512,256]{1,0:T(8,128)(2,1)S(1)}) custom-call(s32[1]{0:T(128)S(6)} %copy.16.turn, s32[2,8]{1,0:T(2,128)} %bitcast.19, s32[256,256]{1,0:T(8,128)} %wedge_hbm.1, bf16[512,256]{1,0:T(8,128)(2,1)} %constant.14.clone.high_hbm, bf16[512,256]{1,0:T(8,128)(2,1)} %constant.15.clone.low_hbm), custom_call_target="tpu_custom_call" | custom-call | flops 200000000 | bytes 3000000 | tf_op jit(solution)/shard_map/pallas_call | solution.py:244
  25.7 1.8 %all-to-all-done = f32[32,4,128]{2,1,0:T(4,128)S(1)} async-done(((f32[32,4,128]{2,1,0:T(4,128)}), f32[32,4,128]{2,1,0:T(4,128)S(1)}, u32[]{:S(2)}, u32[]{:S(2)}) %all-to-all-start) | async-done | bytes 65568 | tf_op jit(solution)/shard_map/all_to_all | solution.py:224
  27.5 0.8 %shard_map.115 = f32[128,128]{1,0:T(8,128)S(1)} custom-call(f32[128,128]{1,0:T(8,128)S(1)} %bitcast.12, f32[256,128]{1,0:T(8,128)S(1)} %get-tuple-element.16.factors, bf16[512,256]{1,0:T(8,128)(2,1)S(1)} %get-tuple-element.17.along_high, bf16[512,256]{1,0:T(8,128)(2,1)S(1)} %get-tuple-element.18.along_low), custom_call_target="tpu_custom_call" | custom-call | flops 200000000 | bytes 2000000 | tf_op jit(solution)/shard_map/pallas_call | solution.py:252
  28.2 15.5 %all_to_all.20 = f32[32,4,128]{2,1,0:T(4,128)S(1)} all-to-all(f32[32,4,128]{2,1,0:T(4,128)S(1)} %bitcast.14), channel_id=1, replica_groups={{16,17,18,19,20,21,22,23,24,25,26,27,28,29,30,31,0,1,2,3,4,5,6,7,8,9,10..., dimensions={0} | all-to-all | bytes 131072 | tf_op jit(solution)/shard_map/all_to_all | solution.py:224
  43.8 1.0 %shard_map.116 = (f32[64,256]{1,0:T(8,128)}, f32[32,128]{1,0:T(8,128)S(1)}) custom-call(f32[128,128]{1,0:T(8,128)S(1)} %bitcast.13, bf16[4096,256]{1,0:T(8,128)(2,1)S(1)} %get-tuple-element.19.features, bf16[256,256]{1,0:T(8,128)(2,1)S(1)} %get-tuple-element.20.fwd_high, bf16[256,256]{1,0:T(8,128)(2,1)S(1)} %get-tuple-element.21.fwd_low), custom_call_target="tpu_custom_call" | custom-call | flops 200000000 | bytes 3000000 | tf_op jit(solution)/shard_map/pallas_call | solution.py:258
  44.8 16.5 %all_to_all.21 = f32[32,1,128]{2,1,0:T(1,128)S(1)} all-to-all(f32[32,1,128]{2,1,0:T(1,128)S(1)} %bitcast.15), channel_id=1, replica_groups={{48,50,52,54,56,58,60,62,0,2,4,6,8,10,12,14,16,18,20,22,24,26,28,30,32,..., dimensions={0} | all-to-all | bytes 32768 | tf_op jit(solution)/shard_map/all_to_all | solution.py:224
  61.3 0.1 reduce_sum.18
  61.4 9.0 %all_to_all.22 = f32[16,1,128]{2,1,0:T(1,128)S(1)} all-to-all(f32[16,1,128]{2,1,0:T(1,128)S(1)} %broadcast_in_dim.2), channel_id=1, replica_groups={{320,321,384,385,448,449,0,1,64,65,128,129,192,193,256,257},{322,323,38..., dimensions={0} | all-to-all | bytes 16384 | tf_op jit(solution)/shard_map/all_to_all | solution.py:224
  70.3 0.5 slice_multiply_fusion
  (2 shorter events, 0.0 us)
Async XLA Ops:
  3.4 24.1 %all-to-all-start = ((f32[32,4,128]{2,1,0:T(4,128)}), f32[32,4,128]{2,1,0:T(4,128)S(1)}, u32[]{:S(2)}, u32[]{:S(2)}) async-start(f32[32,4,128]{2,1,0:T(4,128)} %bitcast.2), calls=%async_computation | async-start | bytes 131072 | tf_op jit(solution)/shard_map/all_to_all | solution.py:224

commit v11 on v10

--- a/solution.py
+++ b/solution.py
@@ -219,9 +219,21 @@
     )
 
 
-def exchange(array, names, size, first):
-    order = [[(first + n) % size for n in range(size)]]
-    return lax.all_to_all(array, names, 0, 0, axis_index_groups=order, tiled=True)
+def turned_order(size, first):
+    return [(first + n) % size for n in range(size)]
+
+
+def far_first(names, sizes, first):
+    dims = [sizes[name] for name in names]
+    spots = np.stack(np.unravel_index(np.arange(math.prod(dims)), dims), 1)
+    apart = np.abs(spots - spots[first])
+    apart = np.minimum(apart, np.array(dims) - apart).sum(1)
+    apart[first] = sum(dims)
+    return [int(n) for n in np.argsort(-apart, kind="stable")]
+
+
+def exchange(array, names, order):
+    return lax.all_to_all(array, names, 0, 0, axis_index_groups=[order], tiled=True)
 
 
 def hbm(array):
@@ -248,11 +260,11 @@
         [pltpu.SMEM((2, NB), jnp.int32), pltpu.VMEM((N, N), jnp.int32), pltpu.SemaphoreType.DMA((4,))],
         (200_000_000, 3_000_000),
     )(rotation, hbm(blocks.T), hbm(wedge), along_high, along_low)
-    lines = exchange(lines.reshape(SLABS, 4, 128), slab, SLABS, HALF).reshape(128, 128)
+    lines = exchange(lines.reshape(SLABS, 4, 128), slab, turned_order(SLABS, HALF)).reshape(128, 128)
     (back,) = call(filter_z, [((128, 128), F32)], "vvvv>v", (), (200_000_000, 2_000_000))(
         lines, factors, along_high, along_low
     )
-    back = exchange(back.reshape(SLABS, 4, 128), slab, SLABS, HALF).reshape(128, 128)
+    back = exchange(back.reshape(SLABS, 4, 128), slab, turned_order(SLABS, HALF)).reshape(128, 128)
     far = math.prod(sizes[name] for name in FAR)
     near = math.prod(sizes[name] for name in NEAR)
     volume, sums = call(
@@ -262,10 +274,10 @@
         [pltpu.VMEM((ROWS, N), F32), pltpu.VMEM((C * YP, 128), F32), pltpu.SemaphoreType.DMA],
         (200_000_000, 3_000_000),
     )(back, features, fwd_high, fwd_low)
-    sums = exchange(sums.reshape(far, 1, 128), FAR, far, FIRST_FAR % far)
+    sums = exchange(sums.reshape(far, 1, 128), FAR, far_first(FAR, sizes, FIRST_FAR % far))
     sums = jnp.sum(sums, 0, keepdims=True)
     sums = jnp.broadcast_to(sums, (near, 1, 128))
-    sums = exchange(sums, NEAR, near, FIRST_NEAR % near)
+    sums = exchange(sums, NEAR, far_first(NEAR, sizes, FIRST_NEAR % near))
     w_grad = jnp.sum(sums, (0, 1))[:C] * (1.0 / (math.prod(sizes.values()) * ROWS * N))
     return volume.reshape(1, ZL, YP, N), w_grad
 

time: 71.7 us -> 71.6 us (level)
  no operation moved by 1% of the time
where the time goes in v11:
time: 71.6 us; the launch traced here: 70.8 us
  blocking collectives  41 us (57%)
  starting transfers between devices  20.2 us (28%)
  Pallas kernels  6 us (8%)
  waiting for transfers between devices  1.77 us (2%)
  between operations  1.32 us (2%)
    all_to_all x3, blocking collectives, exchange(): lax.all_to_all(array, names, 0, 0, axis_index_groups=[order], tiled=True)  41 us
    all_to_all x1, starting transfers between devices, exchange(): lax.all_to_all(array, names, 0, 0, axis_index_groups=[order], tiled=True)  20.2 us
    pallas_call x1, Pallas kernels, on_device(): call(forward_x, [((128, 128), F32), ((C * ROWS, N), BF16), (fwd_high.shap...  2.71 us
    all_to_all x1, waiting for transfers between devices, exchange(): lax.all_to_all(array, names, 0, 0, axis_index_groups=[order], tiled=True)  1.77 us
    pallas_call x1, Pallas kernels, on_device(): call(prepare, [((N, 128), F32), (along_high.shape, BF16), (along_low.shap...  1.48 us
  transfers between devices with their start and end apart: 1, of which 1 were waited for; matrix products, arithmetic and copies ran while one was open for 0% of the time, Pallas kernels for 2%

profile of v11, /device:TPU:1, one launch (start us, length us, event | category | flops | bytes accessed | tf_op | source)
XLA Modules:
  0.0 70.8 jit_solution(11687306849795892220)
XLA Ops:
  0.6 2.7 %shard_map.113 = (f32[128,128]{1,0:T(8,128)}, bf16[4096,256]{1,0:T(8,128)(2,1)S(1)}, bf16[256,256]{1,0:T(8,128)(2,1)S(1)}, bf16[256,256]{1,0:T(8,128)(2,1)S(1)}) custom-call(f32[64]{0:T(128)} %weight_hbm.1, bf16[64,256]{1,0:T(8,128)(2,1)} %bitcast.18, bf16[4096,256]{1,0:T(8,128)(2,1)} %bitcast.16, bf16[256,256]{1,0:T(8,128)(2,1)} %constant.12.clone.high_hbm, ...), custom_call_target="tpu_custom_call" | custom-call | flops 200000000 | bytes 3000000 | tf_op jit(solution)/shard_map/pallas_call | solution.py:248
  3.4 20.2 %all-to-all-start = ((f32[32,4,128]{2,1,0:T(4,128)}), f32[32,4,128]{2,1,0:T(4,128)S(1)}, u32[]{:S(2)}, u32[]{:S(2)}) async-start(f32[32,4,128]{2,1,0:T(4,128)} %bitcast.2), calls=%async_computation | async-start | bytes 131072 | tf_op jit(solution)/shard_map/all_to_all | solution.py:236
  24.2 1.5 %shard_map.114 = (f32[256,128]{1,0:T(8,128)S(1)}, bf16[512,256]{1,0:T(8,128)(2,1)S(1)}, bf16[512,256]{1,0:T(8,128)(2,1)S(1)}) custom-call(s32[1]{0:T(128)S(6)} %copy.16.turn, s32[2,8]{1,0:T(2,128)} %bitcast.19, s32[256,256]{1,0:T(8,128)} %wedge_hbm.1, bf16[512,256]{1,0:T(8,128)(2,1)} %constant.14.clone.high_hbm, bf16[512,256]{1,0:T(8,128)(2,1)} %constant.15.clone.low_hbm), custom_call_target="tpu_custom_call" | custom-call | flops 200000000 | bytes 3000000 | tf_op jit(solution)/shard_map/pallas_call | solution.py:256
  25.7 1.8 %all-to-all-done = f32[32,4,128]{2,1,0:T(4,128)S(1)} async-done(((f32[32,4,128]{2,1,0:T(4,128)}), f32[32,4,128]{2,1,0:T(4,128)S(1)}, u32[]{:S(2)}, u32[]{:S(2)}) %all-to-all-start) | async-done | bytes 65568 | tf_op jit(solution)/shard_map/all_to_all | solution.py:236
  27.5 0.8 %shard_map.115 = f32[128,128]{1,0:T(8,128)S(1)} custom-call(f32[128,128]{1,0:T(8,128)S(1)} %bitcast.12, f32[256,128]{1,0:T(8,128)S(1)} %get-tuple-element.16.factors, bf16[512,256]{1,0:T(8,128)(2,1)S(1)} %get-tuple-element.17.along_high, bf16[512,256]{1,0:T(8,128)(2,1)S(1)} %get-tuple-element.18.along_low), custom_call_target="tpu_custom_call" | custom-call | flops 200000000 | bytes 2000000 | tf_op jit(solution)/shard_map/pallas_call | solution.py:264
  28.2 15.5 %all_to_all.20 = f32[32,4,128]{2,1,0:T(4,128)S(1)} all-to-all(f32[32,4,128]{2,1,0:T(4,128)S(1)} %bitcast.14), channel_id=1, replica_groups={{16,17,18,19,20,21,22,23,24,25,26,27,28,29,30,31,0,1,2,3,4,5,6,7,8,9,10..., dimensions={0} | all-to-all | bytes 131072 | tf_op jit(solution)/shard_map/all_to_all | solution.py:236
  43.8 1.0 %shard_map.116 = (f32[64,256]{1,0:T(8,128)}, f32[32,128]{1,0:T(8,128)S(1)}) custom-call(f32[128,128]{1,0:T(8,128)S(1)} %bitcast.13, bf16[4096,256]{1,0:T(8,128)(2,1)S(1)} %get-tuple-element.19.features, bf16[256,256]{1,0:T(8,128)(2,1)S(1)} %get-tuple-element.20.fwd_high, bf16[256,256]{1,0:T(8,128)(2,1)S(1)} %get-tuple-element.21.fwd_low), custom_call_target="tpu_custom_call" | custom-call | flops 200000000 | bytes 3000000 | tf_op jit(solution)/shard_map/pallas_call | solution.py:270
  44.8 16.4 %all_to_all.21 = f32[32,1,128]{2,1,0:T(1,128)S(1)} all-to-all(f32[32,1,128]{2,1,0:T(1,128)S(1)} %bitcast.15), channel_id=1, replica_groups={{48,0,2,30,32,4,28,34,62,6,26,36,60,8,24,38,58,10,22,40,56,12,20,42,54,..., dimensions={0} | all-to-all | bytes 32768 | tf_op jit(solution)/shard_map/all_to_all | solution.py:236
  61.3 0.1 reduce_sum.18
  61.3 9.0 %all_to_all.22 = f32[16,1,128]{2,1,0:T(1,128)S(1)} all-to-all(f32[16,1,128]{2,1,0:T(1,128)S(1)} %broadcast_in_dim.2), channel_id=1, replica_groups={{320,1,0,65,129,385,64,128,193,257,384,449,192,256,321,448},{322,3,2,67..., dimensions={0} | all-to-all | bytes 16384 | tf_op jit(solution)/shard_map/all_to_all | solution.py:236
  70.3 0.5 slice_multiply_fusion
  (2 shorter events, 0.0 us)
Async XLA Ops:
  3.4 24.1 %all-to-all-start = ((f32[32,4,128]{2,1,0:T(4,128)}), f32[32,4,128]{2,1,0:T(4,128)S(1)}, u32[]{:S(2)}, u32[]{:S(2)}) async-start(f32[32,4,128]{2,1,0:T(4,128)} %bitcast.2), calls=%async_computation | async-start | bytes 131072 | tf_op jit(solution)/shard_map/all_to_all | solution.py:236

commit v12 on v11

--- a/solution.py
+++ b/solution.py
@@ -22,7 +22,7 @@
 PARTS = {"dp": (("y", 4), ("xh", 2), ("core", 2)), "slab": (("z", 16), ("xl", 2))}
 NEAR = ("y", "xh", "xl")
 FAR = ("core", "z")
-HALF = SLABS // 2
+TURN = SLABS // 2 + 1
 FIRST_FAR = 24
 FIRST_NEAR = 10
 
@@ -40,12 +40,12 @@
     step = 2.0 * math.pi / N
     space = np.arange(N)
     quad, slab = np.meshgrid(np.arange(4), np.arange(SLABS), indexing="ij")
-    freq = (4 * ((slab + HALF) % SLABS) + quad).reshape(-1)
+    freq = (4 * ((slab + TURN) % SLABS) + quad).reshape(-1)
     phase = (freq[:, None] * space[None, :]) % N * step
     real, imag = np.cos(phase), -np.sin(phase)
     imag[freq == 0] = np.cos(math.pi * space)
     zp, m, i = np.meshgrid(np.arange(2), np.arange(4), np.arange(SLABS), indexing="ij")
-    depth = (8 * ((i + HALF) % SLABS) + 2 * m + zp).reshape(-1)
+    depth = (8 * ((i + TURN) % SLABS) + 2 * m + zp).reshape(-1)
     phase = (depth[:, None] * depth[None, :]) % N * step
     along = np.concatenate([np.cos(phase), np.sin(phase)], 0)
     return halves(np.concatenate([real, imag], 0)) + halves(along)
@@ -101,7 +101,7 @@
     direct = jnp.where(odd, other[:, 128:], plain[:, :128])
     mirror = jnp.where(odd, other[:, :128], plain[:, 128:]).astype(BF16)
     r = lax.broadcasted_iota(jnp.int32, (N, N), 0)
-    p = (8 * ((r & 31) + HALF) + 2 * ((r >> 5) & 3) + (r >> 7)) & (N - 1)
+    p = (8 * ((r & 31) + TURN) + 2 * ((r >> 5) & 3) + (r >> 7)) & (N - 1)
     k = lane_of((N, N))
     keep = (k == p).astype(F32).astype(BF16)
     flip = (((p + k) & (N - 1)) == 0).astype(F32).astype(BF16)
@@ -178,7 +178,7 @@
     blocks = [lines[pl.ds(m, SLABS, stride=4), :] for m in range(4)]
     line = jnp.concatenate([regroup(blocks, q) for q in range(4)], 0).T
     line = jnp.concatenate([line[:64], line[64:]], 1)
-    line = line * jnp.where((lane_of((ROWS, N)) & 127) == HALF, 1.0 / (N * N), 2.0 / (N * N))
+    line = line * jnp.where((lane_of((ROWS, N)) & 127) == SLABS - TURN, 1.0 / (N * N), 2.0 / (N * N))
     high, low = split(line)
     both = dot(jnp.concatenate([high, low], 0), fwd_high[...])
     values = both[:ROWS] + (both[ROWS:] + dot(high, fwd_low[...]))
@@ -260,11 +260,11 @@
         [pltpu.SMEM((2, NB), jnp.int32), pltpu.VMEM((N, N), jnp.int32), pltpu.SemaphoreType.DMA((4,))],
         (200_000_000, 3_000_000),
     )(rotation, hbm(blocks.T), hbm(wedge), along_high, along_low)
-    lines = exchange(lines.reshape(SLABS, 4, 128), slab, turned_order(SLABS, HALF)).reshape(128, 128)
+    lines = exchange(lines.reshape(SLABS, 4, 128), slab, turned_order(SLABS, TURN)).reshape(128, 128)
     (back,) = call(filter_z, [((128, 128), F32)], "vvvv>v", (), (200_000_000, 2_000_000))(
         lines, factors, along_high, along_low
     )
-    back = exchange(back.reshape(SLABS, 4, 128), slab, turned_order(SLABS, HALF)).reshape(128, 128)
+    back = exchange(back.reshape(SLABS, 4, 128), slab, turned_order(SLABS, TURN)).reshape(128, 128)
     far = math.prod(sizes[name] for name in FAR)
     near = math.prod(sizes[name] for name in NEAR)
     volume, sums = call(

time: 71.6 us -> 71.5 us (level)
  no operation moved by 1% of the time
where the time goes in v12:
time: 71.5 us; the launch traced here: 70.6 us
  blocking collectives  41.3 us (58%)
  starting transfers between devices  20.2 us (28%)
  Pallas kernels  5.99 us (8%)
  between operations  1.32 us (2%)
  waiting for transfers between devices  1.18 us (2%)
    all_to_all x3, blocking collectives, exchange(): lax.all_to_all(array, names, 0, 0, axis_index_groups=[order], tiled=True)  41.3 us
    all_to_all x1, starting transfers between devices, exchange(): lax.all_to_all(array, names, 0, 0, axis_index_groups=[order], tiled=True)  20.2 us
    pallas_call x1, Pallas kernels, on_device(): call(forward_x, [((128, 128), F32), ((C * ROWS, N), BF16), (fwd_high.shap...  2.71 us
    pallas_call x1, Pallas kernels, on_device(): call(prepare, [((N, 128), F32), (along_high.shape, BF16), (along_low.shap...  1.48 us
  transfers between devices with their start and end apart: 1, of which 1 were waited for; matrix products, arithmetic and copies ran while one was open for 0% of the time, Pallas kernels for 2%

profile of v12, /device:TPU:1, one launch (start us, length us, event | category | flops | bytes accessed | tf_op | source)
XLA Modules:
  0.0 70.6 jit_solution(10335551615336750710)
XLA Ops:
  0.6 2.7 %shard_map.113 = (f32[128,128]{1,0:T(8,128)}, bf16[4096,256]{1,0:T(8,128)(2,1)S(1)}, bf16[256,256]{1,0:T(8,128)(2,1)S(1)}, bf16[256,256]{1,0:T(8,128)(2,1)S(1)}) custom-call(f32[64]{0:T(128)} %weight_hbm.1, bf16[64,256]{1,0:T(8,128)(2,1)} %bitcast.18, bf16[4096,256]{1,0:T(8,128)(2,1)} %bitcast.16, bf16[256,256]{1,0:T(8,128)(2,1)} %constant.12.clone.high_hbm, ...), custom_call_target="tpu_custom_call" | custom-call | flops 200000000 | bytes 3000000 | tf_op jit(solution)/shard_map/pallas_call | solution.py:248
  3.4 20.2 %all-to-all-start = ((f32[32,4,128]{2,1,0:T(4,128)}), f32[32,4,128]{2,1,0:T(4,128)S(1)}, u32[]{:S(2)}, u32[]{:S(2)}) async-start(f32[32,4,128]{2,1,0:T(4,128)} %bitcast.2), calls=%async_computation | async-start | bytes 131072 | tf_op jit(solution)/shard_map/all_to_all | solution.py:236
  24.2 1.5 %shard_map.114 = (f32[256,128]{1,0:T(8,128)S(1)}, bf16[512,256]{1,0:T(8,128)(2,1)S(1)}, bf16[512,256]{1,0:T(8,128)(2,1)S(1)}) custom-call(s32[1]{0:T(128)S(6)} %copy.16.turn, s32[2,8]{1,0:T(2,128)} %bitcast.19, s32[256,256]{1,0:T(8,128)} %wedge_hbm.1, bf16[512,256]{1,0:T(8,128)(2,1)} %constant.14.clone.high_hbm, bf16[512,256]{1,0:T(8,128)(2,1)} %constant.15.clone.low_hbm), custom_call_target="tpu_custom_call" | custom-call | flops 200000000 | bytes 3000000 | tf_op jit(solution)/shard_map/pallas_call | solution.py:256
  25.7 1.2 %all-to-all-done = f32[32,4,128]{2,1,0:T(4,128)S(1)} async-done(((f32[32,4,128]{2,1,0:T(4,128)}), f32[32,4,128]{2,1,0:T(4,128)S(1)}, u32[]{:S(2)}, u32[]{:S(2)}) %all-to-all-start) | async-done | bytes 65568 | tf_op jit(solution)/shard_map/all_to_all | solution.py:236
  26.9 0.8 %shard_map.115 = f32[128,128]{1,0:T(8,128)S(1)} custom-call(f32[128,128]{1,0:T(8,128)S(1)} %bitcast.12, f32[256,128]{1,0:T(8,128)S(1)} %get-tuple-element.16.factors, bf16[512,256]{1,0:T(8,128)(2,1)S(1)} %get-tuple-element.17.along_high, bf16[512,256]{1,0:T(8,128)(2,1)S(1)} %get-tuple-element.18.along_low), custom_call_target="tpu_custom_call" | custom-call | flops 200000000 | bytes 2000000 | tf_op jit(solution)/shard_map/pallas_call | solution.py:264
  27.7 15.3 %all_to_all.20 = f32[32,4,128]{2,1,0:T(4,128)S(1)} all-to-all(f32[32,4,128]{2,1,0:T(4,128)S(1)} %bitcast.14), channel_id=1, replica_groups={{17,18,19,20,21,22,23,24,25,26,27,28,29,30,31,0,1,2,3,4,5,6,7,8,9,10,11..., dimensions={0} | all-to-all | bytes 131072 | tf_op jit(solution)/shard_map/all_to_all | solution.py:236
  43.0 1.0 %shard_map.116 = (f32[64,256]{1,0:T(8,128)}, f32[32,128]{1,0:T(8,128)S(1)}) custom-call(f32[128,128]{1,0:T(8,128)S(1)} %bitcast.13, bf16[4096,256]{1,0:T(8,128)(2,1)S(1)} %get-tuple-element.19.features, bf16[256,256]{1,0:T(8,128)(2,1)S(1)} %get-tuple-element.20.fwd_high, bf16[256,256]{1,0:T(8,128)(2,1)S(1)} %get-tuple-element.21.fwd_low), custom_call_target="tpu_custom_call" | custom-call | flops 200000000 | bytes 3000000 | tf_op jit(solution)/shard_map/pallas_call | solution.py:270
  44.0 16.5 %all_to_all.21 = f32[32,1,128]{2,1,0:T(1,128)S(1)} all-to-all(f32[32,1,128]{2,1,0:T(1,128)S(1)} %bitcast.15), channel_id=1, replica_groups={{48,0,2,30,32,4,28,34,62,6,26,36,60,8,24,38,58,10,22,40,56,12,20,42,54,..., dimensions={0} | all-to-all | bytes 32768 | tf_op jit(solution)/shard_map/all_to_all | solution.py:236
  60.6 0.1 reduce_sum.18
  60.6 9.5 %all_to_all.22 = f32[16,1,128]{2,1,0:T(1,128)S(1)} all-to-all(f32[16,1,128]{2,1,0:T(1,128)S(1)} %broadcast_in_dim.2), channel_id=1, replica_groups={{320,1,0,65,129,385,64,128,193,257,384,449,192,256,321,448},{322,3,2,67..., dimensions={0} | all-to-all | bytes 16384 | tf_op jit(solution)/shard_map/all_to_all | solution.py:236
  70.1 0.5 slice_multiply_fusion
  (2 shorter events, 0.0 us)
Async XLA Ops:
  3.4 23.5 %all-to-all-start = ((f32[32,4,128]{2,1,0:T(4,128)}), f32[32,4,128]{2,1,0:T(4,128)S(1)}, u32[]{:S(2)}, u32[]{:S(2)}) async-start(f32[32,4,128]{2,1,0:T(4,128)} %bitcast.2), calls=%async_computation | async-start | bytes 131072 | tf_op jit(solution)/shard_map/all_to_all | solution.py:236

commit v13 on v12

--- a/solution.py
+++ b/solution.py
@@ -24,7 +24,7 @@
 FAR = ("core", "z")
 TURN = SLABS // 2 + 1
 FIRST_FAR = 24
-FIRST_NEAR = 10
+FIRST_NEAR = 11
 
 F32, BF16 = jnp.float32, jnp.bfloat16
 VMEM_LIMIT = 16 * 1024 * 1024

time: 71.5 us -> 72 us (level)
  no operation moved by 1% of the time
where the time goes in v13:
time: 72 us; the launch traced here: 71.2 us
  blocking collectives  41.9 us (58%)
  starting transfers between devices  20.2 us (28%)
  Pallas kernels  5.99 us (8%)
  between operations  1.32 us (2%)
  waiting for transfers between devices  1.18 us (2%)
    all_to_all x3, blocking collectives, exchange(): lax.all_to_all(array, names, 0, 0, axis_index_groups=[order], tiled=True)  41.9 us
    all_to_all x1, starting transfers between devices, exchange(): lax.all_to_all(array, names, 0, 0, axis_index_groups=[order], tiled=True)  20.2 us
    pallas_call x1, Pallas kernels, on_device(): call(forward_x, [((128, 128), F32), ((C * ROWS, N), BF16), (fwd_high.shap...  2.71 us
    pallas_call x1, Pallas kernels, on_device(): call(prepare, [((N, 128), F32), (along_high.shape, BF16), (along_low.shap...  1.48 us
  transfers between devices with their start and end apart: 1, of which 1 were waited for; matrix products, arithmetic and copies ran while one was open for 0% of the time, Pallas kernels for 2%

profile of v13, /device:TPU:1, one launch (start us, length us, event | category | flops | bytes accessed | tf_op | source)
XLA Modules:
  0.0 71.2 jit_solution(5569520571309588845)
XLA Ops:
  0.6 2.7 %shard_map.113 = (f32[128,128]{1,0:T(8,128)}, bf16[4096,256]{1,0:T(8,128)(2,1)S(1)}, bf16[256,256]{1,0:T(8,128)(2,1)S(1)}, bf16[256,256]{1,0:T(8,128)(2,1)S(1)}) custom-call(f32[64]{0:T(128)} %weight_hbm.1, bf16[64,256]{1,0:T(8,128)(2,1)} %bitcast.18, bf16[4096,256]{1,0:T(8,128)(2,1)} %bitcast.16, bf16[256,256]{1,0:T(8,128)(2,1)} %constant.12.clone.high_hbm, ...), custom_call_target="tpu_custom_call" | custom-call | flops 200000000 | bytes 3000000 | tf_op jit(solution)/shard_map/pallas_call | solution.py:248
  3.4 20.2 %all-to-all-start = ((f32[32,4,128]{2,1,0:T(4,128)}), f32[32,4,128]{2,1,0:T(4,128)S(1)}, u32[]{:S(2)}, u32[]{:S(2)}) async-start(f32[32,4,128]{2,1,0:T(4,128)} %bitcast.2), calls=%async_computation | async-start | bytes 131072 | tf_op jit(solution)/shard_map/all_to_all | solution.py:236
  24.2 1.5 %shard_map.114 = (f32[256,128]{1,0:T(8,128)S(1)}, bf16[512,256]{1,0:T(8,128)(2,1)S(1)}, bf16[512,256]{1,0:T(8,128)(2,1)S(1)}) custom-call(s32[1]{0:T(128)S(6)} %copy.16.turn, s32[2,8]{1,0:T(2,128)} %bitcast.19, s32[256,256]{1,0:T(8,128)} %wedge_hbm.1, bf16[512,256]{1,0:T(8,128)(2,1)} %constant.14.clone.high_hbm, bf16[512,256]{1,0:T(8,128)(2,1)} %constant.15.clone.low_hbm), custom_call_target="tpu_custom_call" | custom-call | flops 200000000 | bytes 3000000 | tf_op jit(solution)/shard_map/pallas_call | solution.py:256
  25.7 1.2 %all-to-all-done = f32[32,4,128]{2,1,0:T(4,128)S(1)} async-done(((f32[32,4,128]{2,1,0:T(4,128)}), f32[32,4,128]{2,1,0:T(4,128)S(1)}, u32[]{:S(2)}, u32[]{:S(2)}) %all-to-all-start) | async-done | bytes 65568 | tf_op jit(solution)/shard_map/all_to_all | solution.py:236
  26.9 0.8 %shard_map.115 = f32[128,128]{1,0:T(8,128)S(1)} custom-call(f32[128,128]{1,0:T(8,128)S(1)} %bitcast.12, f32[256,128]{1,0:T(8,128)S(1)} %get-tuple-element.16.factors, bf16[512,256]{1,0:T(8,128)(2,1)S(1)} %get-tuple-element.17.along_high, bf16[512,256]{1,0:T(8,128)(2,1)S(1)} %get-tuple-element.18.along_low), custom_call_target="tpu_custom_call" | custom-call | flops 200000000 | bytes 2000000 | tf_op jit(solution)/shard_map/pallas_call | solution.py:264
  27.7 15.3 %all_to_all.20 = f32[32,4,128]{2,1,0:T(4,128)S(1)} all-to-all(f32[32,4,128]{2,1,0:T(4,128)S(1)} %bitcast.14), channel_id=1, replica_groups={{17,18,19,20,21,22,23,24,25,26,27,28,29,30,31,0,1,2,3,4,5,6,7,8,9,10,11..., dimensions={0} | all-to-all | bytes 131072 | tf_op jit(solution)/shard_map/all_to_all | solution.py:236
  43.0 1.0 %shard_map.116 = (f32[64,256]{1,0:T(8,128)}, f32[32,128]{1,0:T(8,128)S(1)}) custom-call(f32[128,128]{1,0:T(8,128)S(1)} %bitcast.13, bf16[4096,256]{1,0:T(8,128)(2,1)S(1)} %get-tuple-element.19.features, bf16[256,256]{1,0:T(8,128)(2,1)S(1)} %get-tuple-element.20.fwd_high, bf16[256,256]{1,0:T(8,128)(2,1)S(1)} %get-tuple-element.21.fwd_low), custom_call_target="tpu_custom_call" | custom-call | flops 200000000 | bytes 3000000 | tf_op jit(solution)/shard_map/pallas_call | solution.py:270
  44.0 16.5 %all_to_all.21 = f32[32,1,128]{2,1,0:T(1,128)S(1)} all-to-all(f32[32,1,128]{2,1,0:T(1,128)S(1)} %bitcast.15), channel_id=1, replica_groups={{48,0,2,30,32,4,28,34,62,6,26,36,60,8,24,38,58,10,22,40,56,12,20,42,54,..., dimensions={0} | all-to-all | bytes 32768 | tf_op jit(solution)/shard_map/all_to_all | solution.py:236
  60.6 0.1 reduce_sum.18
  60.6 10.0 %all_to_all.22 = f32[16,1,128]{2,1,0:T(1,128)S(1)} all-to-all(f32[16,1,128]{2,1,0:T(1,128)S(1)} %broadcast_in_dim.2), channel_id=1, replica_groups={{321,0,1,64,128,384,65,129,192,256,385,448,193,257,320,449},{323,2,3,66..., dimensions={0} | all-to-all | bytes 16384 | tf_op jit(solution)/shard_map/all_to_all | solution.py:236
  70.7 0.5 slice_multiply_fusion
  (2 shorter events, 0.0 us)
Async XLA Ops:
  3.4 23.5 %all-to-all-start = ((f32[32,4,128]{2,1,0:T(4,128)}), f32[32,4,128]{2,1,0:T(4,128)S(1)}, u32[]{:S(2)}, u32[]{:S(2)}) async-start(f32[32,4,128]{2,1,0:T(4,128)} %bitcast.2), calls=%async_computation | async-start | bytes 131072 | tf_op jit(solution)/shard_map/all_to_all | solution.py:236
